TPU v7x, 512 devices: a whole 4x4x16 slice. The times are simulated.
512 devices in a mesh: users: 128 (over z, x, core), items: 4 (over y).
Axes of the slice: x: 4, y: 4, z: 16, core: 2. Of those that a mesh axis runs over, the one named last changes fastest.
Arguments:
- tile_users: int32 [128, 4, 128], P('users', 'items'), may hold values from 0 to 127
- tile_owners: int32 [128, 4, 128, 1], P('users', 'items'), may hold values from 0 to 127; in each aligned block of 128 rows (0 to 127, 128 to 255, ..., all dimensions but the last counted through in order) at most 2 rows name the same one
- tile_blocks: int32 [128, 4, 128], P('users', 'items'), may hold values from 0 to 3
- tile_contexts: int32 [128, 4, 128], P('users', 'items'), may hold values from 0 to 7
- row_users: int32 [128, 4, 128, 128], P('users', 'items'), may hold values from 0 to 15
- row_items: int32 [128, 4, 128, 128], P('users', 'items'), may hold values from 0 to 15
- row_contexts: int32 [128, 4, 128, 128], P('users', 'items'), may hold values from 0 to 127
- tile_values: bfloat16 [128, 4, 128, 128], P('users', 'items'), may hold values from -49152 to 49152
- tile_count: int32 [128, 4], P('users', 'items'), may hold values from 64 to 128, as said below
- item_factors: bfloat16 [8192, 256], P('users'), may hold values from -0.125 to 0.25
- context_factors: bfloat16 [1024, 256], replicated, may hold values from -0.125 to 0.25
- profile: bfloat16 [262144, 2048], P('users', 'items'), may hold values from -192 to 192
- feature_factors: bfloat16 [2048, 256], P('items'), may hold values from -6 to 6
Outputs:
- user_factors: bfloat16 [262144, 256], P('users')
- feature_new: bfloat16 [2048, 256], P('items')
Inputs may be any that keep to these rules, and one draw needn't show every extreme that they name: On one device at most 2 tiles name one index of users in tile_owners, a bound that some block reaches. The live tiles of a device are its first tile_count tiles; some device has all 128 live.
All inputs are finite; a program needn't handle non-finite values.
Results may differ from a plain program's by a relative error of at most 0.00155.
The roundings to bfloat16 on the way count: a program that leaves them out, or rounds other values in their place, can miss the bound.
Values may be sent and summed in bfloat16 or wider, within the bound.
A program may use at most 64 MiB of HBM per device.

v0:
```python
import jax
import jax.numpy as jnp
from jax import lax
from jax.sharding import PartitionSpec as P

CB = 128
IB = 16
UB = 16


RIDGE = 1.0


def gram(matrix):
    return lax.dot_general(
        matrix, matrix, (((0,), (0,)), ((), ())), preferred_element_type=jnp.float32
    )


def solve_rows(normal, right_side):
    cholesky_factor = jnp.linalg.cholesky(normal)
    return jax.scipy.linalg.cho_solve((cholesky_factor, True), right_side.T).T


def local(
    tile_users,
    tile_owners,
    tile_blocks,
    tile_contexts,
    row_users,
    row_items,
    row_contexts,
    tile_values,
    tile_count,
    item_factors,
    context_factors,
    profile,
    feature_factors,
):
    users_size = lax.axis_size("users")
    tile_total = tile_users.shape[2]
    rank_width = item_factors.shape[1]
    slab_users = profile.shape[0]
    blocks_held = item_factors.shape[0] // IB
    capacity = max(2, 2 * tile_total // users_size)
    owners = tile_owners.reshape(tile_total)
    local_block = tile_blocks.reshape(tile_total)
    live_count = tile_count.reshape(())
    position = jnp.arange(tile_total, dtype=jnp.int32)
    same_owner = (owners[:, None] == owners[None, :]) & (position[None, :] < position[:, None])
    slot_rank = jnp.sum(same_owner.astype(jnp.int32), axis=1)
    tile_place = owners * capacity + slot_rank
    request_block = jnp.where(position < live_count, local_block, 0)
    wanted = jnp.zeros((users_size * capacity,), jnp.int32).at[tile_place].set(request_block)
    asked_blocks = lax.all_to_all(
        wanted.reshape(users_size, capacity), "users", split_axis=0, concat_axis=0, tiled=True
    )
    shard_blocks = item_factors.reshape(blocks_held, IB, rank_width)
    answered = shard_blocks[asked_blocks.reshape(-1)].reshape(users_size, capacity, IB, rank_width)
    fetched = lax.all_to_all(answered, "users", split_axis=0, concat_axis=0, tiled=True).reshape(
        users_size * capacity, IB, rank_width
    )
    identity = jnp.eye(rank_width, dtype=jnp.float32)
    context_gram = gram(context_factors)
    item_gram = lax.psum(gram(item_factors), "users")
    feature_gram = lax.psum(gram(feature_factors), "items")
    normal = item_gram * context_gram + feature_gram
    normal = normal + RIDGE * identity
    user_blocks = slab_users // UB
    context_table = context_factors.reshape(-1, CB, rank_width)
    tile_ublock = tile_users.reshape(tile_total)
    tile_cblock = tile_contexts.reshape(tile_total)
    users_rows = row_users.reshape(tile_total, -1)
    items_rows = row_items.reshape(tile_total, -1)
    contexts_rows = row_contexts.reshape(tile_total, -1)
    values_rows = tile_values.reshape(tile_total, -1)
    group_size = 16

    def add_group(step_index, running):
        first_tile = step_index * group_size

        def window(source):
            return lax.dynamic_slice_in_dim(source, first_tile, group_size, 0)

        item_blocks = fetched[window(tile_place)]
        context_blocks = context_table[window(tile_cblock)]
        item_onehot = (
            window(items_rows)[:, :, None] == jnp.arange(IB, dtype=jnp.int32)[None, None, :]
        ).astype(jnp.bfloat16)
        context_onehot = (
            window(contexts_rows)[:, :, None] == jnp.arange(CB, dtype=jnp.int32)[None, None, :]
        ).astype(jnp.bfloat16)
        item_rows_sel = jnp.einsum(
            "gti,gir->gtr", item_onehot, item_blocks, preferred_element_type=jnp.float32
        )
        context_rows_sel = jnp.einsum(
            "gtc,gcr->gtr", context_onehot, context_blocks, preferred_element_type=jnp.float32
        )
        alive_mask = (first_tile + jnp.arange(group_size, dtype=jnp.int32) < live_count).astype(
            jnp.float32
        )
        weighted = window(values_rows).astype(jnp.float32) * alive_mask[:, None]
        row_terms = weighted[:, :, None] * item_rows_sel * context_rows_sel
        user_onehot = (
            window(users_rows)[:, None, :] == jnp.arange(UB, dtype=jnp.int32)[None, :, None]
        ).astype(jnp.float32)
        per_tile = jnp.einsum(
            "gut,gtr->gur", user_onehot, row_terms, precision=lax.Precision.HIGHEST
        )
        block_onehot = (
            window(tile_ublock)[None, :] == jnp.arange(user_blocks, dtype=jnp.int32)[:, None]
        ).astype(jnp.float32)
        return running + jnp.einsum(
            "bg,gur->bur", block_onehot, per_tile, precision=lax.Precision.HIGHEST
        )

    rounds = (live_count + group_size - 1) // group_size
    mttkrp = lax.fori_loop(
        0, rounds, add_group, jnp.zeros((user_blocks, UB, rank_width), jnp.float32)
    ).reshape(slab_users, rank_width)
    local_right = mttkrp + jnp.dot(profile, feature_factors, preferred_element_type=jnp.float32)
    right_side = lax.psum(local_right, "items")
    user_factors = solve_rows(normal, right_side).astype(jnp.bfloat16)
    feature_terms = lax.dot_general(
        profile, user_factors, (((0,), (0,)), ((), ())), preferred_element_type=jnp.float32
    )
    user_gram, feature_right = lax.psum((gram(user_factors), feature_terms), "users")
    feature_new = solve_rows(user_gram + RIDGE * identity, feature_right).astype(jnp.bfloat16)
    return (user_factors, feature_new)


def solution(mesh):
    in_specs = (
        P("users", "items", None),
        P("users", "items", None, None),
        P("users", "items", None),
        P("users", "items", None),
        P("users", "items", None, None),
        P("users", "items", None, None),
        P("users", "items", None, None),
        P("users", "items", None, None),
        P("users", "items"),
        P("users", None),
        P(),
        P("users", "items"),
        P("items", None),
    )
    out_specs = (P("users", None), P("items", None))
    return jax.shard_map(local, mesh=mesh, in_specs=in_specs, out_specs=out_specs, check_vma=False)
```

profile of v0, /device:TPU:1, one launch (start us, length us, event | category | flops | bytes accessed | tf_op | source)
XLA Modules:
  0.0 968.9 jit_solution(7956895656992182176)
XLA Ops:
  11.3 35.1 %all_to_all.14 = s32[128,1,2]{2,1,0:T(1,128)S(1)} all-to-all(s32[128,1,2]{2,1,0:T(1,128)S(1)} %bitcast.135), channel_id=1, replica_groups=mesh['users'=128,'items'=4] {'users'}, dimensions={0} | all-to-all | bytes 2048 | tf_op jit(solution)/shard_map/all_to_all | solution.py:55
  47.9 2.8 gather_fusion.2
  50.7 6.9 all-to-all-start.1
  59.8 95.1 %all-to-all-done.1 = bf16[128,2,16,256]{3,2,1,0:T(8,128)(2,1)} async-done(((bf16[128,2,16,256]{3,2,1,0:T(8,128)(2,1)}), bf16[128,2,16,256]{3,2,1,0:T(8,128)(2,1)}, u32[]{:S(2)}, u32[]{:S(2)}) %all-to-all-start.1) | async-done | bytes 2097184 | tf_op jit(solution)/shard_map/all_to_all | solution.py:60
  154.9 1.5 broadcast_in_dim.8
  156.4 57.1 %while.12 = (s32[]{:T(128)}, f32[128,16,256]{2,0,1:T(8,128)}, s32[]{:T(128)}, s32[128]{0:T(128)S(1)}, s32[128,128]{1,0:T(8,128)}, /*index=5*/bf16[128,128]{1,0:T...) while((s32[]{:T(128)}, f32[128,16,256]{2,0,1:T(8,128)}, ...), condition=%wide.region_9.11_spmd, body=%wide.region_8.10_spmd.sunk | while | flops 354230400 | bytes 25138244 | solution.py:118
  156.5 1.7 gather_fusion
  158.9 1.8 fusion.91
  160.7 2.2 gather_fusion.1
  166.7 4.0 convolution_add_fusion.3
  170.8 1.7 gather_fusion
  173.2 1.8 fusion.91
  175.0 2.1 gather_fusion.1
  181.0 4.0 convolution_add_fusion.3
  185.0 1.7 gather_fusion
  187.4 1.8 fusion.91
  189.2 2.1 gather_fusion.1
  195.2 4.0 convolution_add_fusion.3
  199.3 1.7 gather_fusion
  201.7 1.8 fusion.91
  203.5 2.1 gather_fusion.1
  209.5 4.0 convolution_add_fusion.3
  213.5 2.8 copy.51
  216.3 2.0 fusion.13
  219.0 192.9 %all-reduce.7.cloned.1.call-done = f32[256,256]{0,1:T(8,128)} async-done(((f32[256,256]{0,1:T(8,128)}), f32[256,256]{0,1:T(8,128)}) %all-reduce.7.cloned.1.call-update) | async-done | bytes 262160 | tf_op jit(solution)/shard_map/psum | solution.py:65
  411.9 79.3 %all-reduce.11.cloned.1.call-done = (f32[256,2048]{0,1:T(8,128)}, f32[256,256]{0,1:T(8,128)}) async-done(((f32[256,2048]{0,1:T(8,128)}, f32[256,256]{0,1:T(8,128)}), (f32[256,2048]{0,1:T(8,128)}, f32[256,256]{0,1:T(8,128)})) %all-reduce.11.cloned.1.call-update) | async-done | bytes 2359312 | tf_op jit(solution)/shard_map/psum | solution.py:122
  491.2 1.4 fusion.15
  492.8 11.7 %cholesky.130 = f32[128,128]{1,0:T(8,128)S(1)} custom-call(f32[128,128]{1,0:T(8,128)S(1)} %cholesky.194), custom_call_target="Cholesky" | custom-call | tf_op jit(solution)/shard_map/jit(cholesky)/cholesky | solution.py:21
  504.6 9.8 %custom-call.25 = f32[1,128,128]{1,2,0:T(8,128)S(1)} custom-call(f32[1,128,128]{2,1,0:T(8,128)S(1)} %get-tuple-element.157), custom_call_target="InvertDiagBlocksLowerTriangular" | custom-call | tf_op jit(solution)/shard_map/jit(cholesky)/cholesky | solution.py:21
  514.8 11.7 %cholesky.147 = f32[128,128]{1,0:T(8,128)S(1)} custom-call(f32[128,128]{1,0:T(8,128)S(1)} %convolution_subtract_fusion.5), custom_call_target="Cholesky" | custom-call | tf_op jit(solution)/shard_map/jit(cholesky)/cholesky | solution.py:21
  528.7 4.2 while.13
  529.4 1.4 bitcast_dynamic-update-slice_fusion.4
  531.4 1.4 bitcast_dynamic-update-slice_fusion.4
  532.8 19.7 %custom-call.22 = f32[2,128,128]{1,2,0:T(8,128)S(1)} custom-call(f32[2,128,128]{2,1,0:T(8,128)S(1)} %get-tuple-element.79), custom_call_target="InvertDiagBlocksLowerTriangular" | custom-call | tf_op jit(solution)/shard_map/jit(_cho_solve)/triangular_solve | solution.py:22
  552.5 2.4 fusion.16
  555.0 1.8 convolution_subtract_fusion.1
  561.0 1.2 fusion.19
  562.2 1.5 fusion.18
  563.8 1.3 fusion.20
  565.0 1.5 copy.55
  566.5 329.8 %all-reduce.9.cloned.1.call-done = (f32[256,512]{1,0:T(8,128)}, f32[256,256]{0,1:T(8,128)}) async-done(((f32[256,512]{1,0:T(8,128)}, f32[256,256]{0,1:T(8,128)}), (f32[256,512]{1,0:T(8,128)}, f32[256,256]{0,1:T(8,128)})) %all-reduce.9.cloned.1.call-update) | async-done | bytes 786448 | tf_op jit(solution)/shard_map/psum | solution.py:127
  898.5 11.7 %cholesky.164 = f32[128,128]{1,0:T(8,128)S(1)} custom-call(f32[128,128]{1,0:T(8,128)S(1)} %cholesky.197), custom_call_target="Cholesky" | custom-call | tf_op jit(solution)/shard_map/jit(cholesky)/cholesky | solution.py:21
  910.2 9.8 %custom-call.26 = f32[1,128,128]{1,2,0:T(8,128)S(1)} custom-call(f32[1,128,128]{2,1,0:T(8,128)S(1)} %get-tuple-element.153), custom_call_target="InvertDiagBlocksLowerTriangular" | custom-call | tf_op jit(solution)/shard_map/jit(cholesky)/cholesky | solution.py:21
  920.5 11.7 %cholesky.181 = f32[128,128]{1,0:T(8,128)S(1)} custom-call(f32[128,128]{1,0:T(8,128)S(1)} %convolution_subtract_fusion.4), custom_call_target="Cholesky" | custom-call | tf_op jit(solution)/shard_map/jit(cholesky)/cholesky | solution.py:21
  934.9 3.9 while.14
  935.5 1.3 bitcast_dynamic-update-slice_fusion.5
  937.5 1.3 bitcast_dynamic-update-slice_fusion.5
  938.8 19.9 %custom-call.23 = f32[2,128,128]{1,2,0:T(8,128)S(1)} custom-call(f32[2,128,128]{2,1,0:T(8,128)S(1)} %get-tuple-element.87), custom_call_target="InvertDiagBlocksLowerTriangular" | custom-call | tf_op jit(solution)/shard_map/jit(_cho_solve)/triangular_solve | solution.py:22
  (135 shorter events, 41.2 us)
Async XLA Ops:
  7.2 209.1 %copy-start = (bf16[2048,512]{1,0:T(8,128)(2,1)S(1)}, bf16[2048,512]{1,0:T(8,128)(2,1)}, u32[]{:S(2)}) copy-start(bf16[2048,512]{1,0:T(8,128)(2,1)} %param.27) | copy-start | bytes 6291460
  50.7 7.0 copy-start.2
  50.7 8.0 copy-start.10
  50.7 8.0 copy-start.4
  50.7 104.1 %all-to-all-start.1 = ((bf16[128,2,16,256]{3,2,1,0:T(8,128)(2,1)}), bf16[128,2,16,256]{3,2,1,0:T(8,128)(2,1)}, u32[]{:S(2)}, u32[]{:S(2)}) async-start(bf16[128,2,16,256]{3,2,1,0:T(8,128)(2,1)} %bitcast.134), calls=%async_computation.1 | async-start | bytes 4194304 | tf_op jit(solution)/shard_map/all_to_all | solution.py:60
  57.6 98.8 %copy-start.9 = (s32[1,1,128]{2,1,0:T(1,128)S(1)}, s32[1,1,128]{2,1,0:T(1,128)}, u32[]{:S(2)}) copy-start(s32[1,1,128]{2,1,0:T(1,128)} %param.19) | copy-start | bytes 1540
  57.7 98.7 %copy-start.11 = (s32[1,1,128]{2,1,0:T(1,128)S(1)}, s32[1,1,128]{2,1,0:T(1,128)}, u32[]{:S(2)}) copy-start(s32[1,1,128]{2,1,0:T(1,128)} %param.16) | copy-start | bytes 1540
  57.7 354.2 %all-reduce.7.cloned.1.call-start = ((), (), s32[]{:S(2)}) async-start(), calls=%async_computation.2 | async-start | bytes 524288 | tf_op jit(solution)/shard_map/psum | solution.py:65
  58.7 432.5 %all-reduce.11.cloned.1.call-start = ((), (), s32[]{:S(2)}) async-start(), calls=%async_computation.4 | async-start | bytes 4718592 | tf_op jit(solution)/shard_map/psum | solution.py:122
  162.8 2.8 copy-start.1
  177.1 2.8 copy-start.1
  191.4 2.8 copy-start.1
  205.7 2.8 copy-start.1
  218.4 272.8 %copy-start.3 = (bf16[8,128,256]{2,1,0:T(8,128)(2,1)S(1)}, bf16[8,128,256]{2,1,0:T(8,128)(2,1)}, u32[]{:S(2)}) copy-start(bf16[8,128,256]{2,1,0:T(8,128)(2,1)} %get-tuple-element.404) | copy-start | bytes 1572868
  218.4 677.9 %all-reduce.9.cloned.1.call-start = ((), (), s32[]{:S(2)}) async-start(), calls=%async_computation.3 | async-start | bytes 1572864 | tf_op jit(solution)/shard_map/psum | solution.py:127
  552.5 2.5 copy-start.5
  558.9 3.3 copy-start.7
  561.0 1.2 copy-start.6
  897.3 61.5 %copy-start.8 = (f32[256,512]{1,0:T(8,128)S(1)}, f32[256,512]{1,0:T(8,128)}, u32[]{:S(2)}) copy-start(f32[256,512]{1,0:T(8,128)} %get-tuple-element.138) | copy-start | bytes 1572868
Sparse Core Ops, SparseCore 0:
  62.5 349.2 all-reduce.6
  414.9 76.2 all-reduce.10
  563.9 332.3 all-reduce.8
where the time goes:
time: 979 us; the launch traced here: 969 us
  waiting for transfers between devices  697 us (71%)
  other arithmetic  121 us (12%)
  matrix products  48.9 us (5%)
  local copies, waits for them, and re-layouts  40.7 us (4%)
  blocking collectives  35.1 us (4%)
  between operations  17.8 us (2%)
    psum x1, waiting for transfers between devices, local(): lax.psum((gram(user_factors), feature_terms), 'users')  330 us
    psum x1, waiting for transfers between devices, local(): item_gram = lax.psum(gram(item_factors), 'users')  193 us
    all_to_all x1, waiting for transfers between devices, local(): lax.all_to_all(answered, 'users', split_axis=0, concat_axis=0, tiled=True)  95.1 us
    psum x1, waiting for transfers between devices, local(): right_side = lax.psum(local_right, 'items')  79.3 us
    another operation x13, other arithmetic, solve_rows(): cholesky_factor = jnp.linalg.cholesky(normal)  68.6 us
    another operation x5, other arithmetic, solve_rows(): return jax.scipy.linalg.cho_solve((cholesky_factor, True), right_side.T).T  39.7 us
    all_to_all x1, blocking collectives, local(): lax.all_to_all(wanted.reshape(users_size, capacity), 'users', split_axis=...  35.1 us
  transfers between devices with their start and end apart: 4, of which 4 were waited for; matrix products, arithmetic and copies ran while one was open for 7% of the time, Pallas kernels for 0%

commit v1 on v0

v1 whole, which is shorter than its diff:
```python
import functools

import jax
import jax.numpy as jnp
from jax import lax
from jax.experimental import pallas as pl
from jax.experimental.pallas import tpu as pltpu
from jax.sharding import PartitionSpec as P

NZ, NX, NC, NY = 16, 4, 2, 4
R = 256
CB, IB, UB, TR = 128, 16, 16, 128
TILES = 128
SLAB = 2048
RIDGE = 1.0
MESH = pl.DeviceIdType.MESH
F32 = jnp.float32
BF16 = jnp.bfloat16
HIGHEST = lax.Precision.HIGHEST
VMEM_LIMIT = 56 * 1024 * 1024


def position():
    u = lax.axis_index("users")
    y = lax.axis_index("items")
    return lax.div(u, 8), lax.rem(lax.div(u, 2), 4), lax.rem(u, 2), y


def neighbour(dz=0, dx=0, dc=0, dy=0):
    z, x, c, y = position()
    zz = lax.rem(z + dz + NZ, NZ)
    xx = lax.rem(x + dx + NX, NX)
    cc = lax.rem(c + dc, NC)
    return (zz * 8 + xx * 2 + cc, lax.rem(y + dy + NY, NY))


def greet(devices):
    barrier = pltpu.get_barrier_semaphore()
    for device in devices:
        pl.semaphore_signal(barrier, inc=1, device_id=device, device_id_type=MESH)
    pl.semaphore_wait(barrier, len(devices))


class Sender:
    def __init__(self, send_sem, recv_sem):
        self.send_sem, self.recv_sem, self.sent = send_sem, recv_sem, []

    def __call__(self, src, dst, device):
        i = len(self.sent)
        copy = pltpu.make_async_remote_copy(
            src_ref=src,
            dst_ref=dst,
            send_sem=self.send_sem.at[i],
            recv_sem=self.recv_sem.at[i],
            device_id=device,
            device_id_type=MESH,
        )
        copy.start()
        self.sent.append(copy)
        return copy

    def finish(self):
        for copy in self.sent:
            copy.wait_send()


def gather_kernel(item_ref, feat_ref, tab, fall, send_sem, recv_sem):
    c = position()[2]
    xp, xm, x2 = neighbour(dx=1), neighbour(dx=-1), neighbour(dx=2)
    zp, zm, sib = neighbour(dz=1), neighbour(dz=-1), neighbour(dc=1)
    yp, ym, y2 = neighbour(dy=1), neighbour(dy=-1), neighbour(dy=2)
    tab[0, 0, 0, 0] = item_ref[0:32, :]
    tab[1, 0, 0, 0] = item_ref[32:64, :]
    greet([xp, xm, x2, zp, zm, sib, yp, ym, y2])
    go = Sender(send_sem, recv_sem)

    own = tab.at[0, 0, 0, 0]
    first = [go(own, tab.at[0, 0, 0, 3], xp), go(own, tab.at[0, 0, 0, 1], xm), go(own, tab.at[0, 0, 0, 2], x2)]

    def ring1(s):
        if s < 7:
            return (
                go(tab.at[1, 0, (-s) % 16, 0], tab.at[1, 0, (-s - 1) % 16, 0], zp),
                go(tab.at[1, 0, s, 0], tab.at[1, 0, s + 1, 0], zm),
            )
        return (
            go(tab.at[1, 0, 9, 0, pl.ds(0, 16)], tab.at[1, 0, 8, 0, pl.ds(0, 16)], zp),
            go(tab.at[1, 0, 7, 0, pl.ds(16, 16)], tab.at[1, 0, 8, 0, pl.ds(16, 16)], zm),
        )

    def ring0(s):
        if s < 7:
            return (
                go(tab.at[0, 0, (-s) % 16], tab.at[0, 0, (-s - 1) % 16], zp),
                go(tab.at[0, 0, s], tab.at[0, 0, s + 1], zm),
            )
        return (
            go(tab.at[0, 0, 9, pl.ds(0, 2)], tab.at[0, 0, 8, pl.ds(0, 2)], zp),
            go(tab.at[0, 0, 7, pl.ds(2, 2)], tab.at[0, 0, 8, pl.ds(2, 2)], zm),
        )

    def cross(lo, n):
        return (
            lo,
            n,
            go(tab.at[1, 0, pl.ds(lo, n), 0], tab.at[1, 0, pl.ds(lo, n), 3], xp),
            go(tab.at[1, 0, pl.ds(lo, n), 0], tab.at[1, 0, pl.ds(lo, n), 1], xm),
        )

    def cross_on(group):
        lo, n, p, m = group
        d = pl.ds(lo, n)
        p.wait_recv()
        a = go(tab.at[1, 0, d, 3, pl.ds(0, 16)], tab.at[1, 0, d, 2, pl.ds(0, 16)], xp)
        m.wait_recv()
        b = go(tab.at[1, 0, d, 1, pl.ds(16, 16)], tab.at[1, 0, d, 2, pl.ds(16, 16)], xm)
        return (lo, n, a, b)

    def share(half, lo, n):
        return go(tab.at[half, 0, pl.ds(lo, n)], tab.at[half, 1, pl.ds(lo, n)], sib)

    shared = []

    def cross_off(group):
        lo, n, a, b = group
        a.wait_recv()
        b.wait_recv()
        shared.append(share(1, lo, n))

    r1 = ring1(0)
    crossing, crossed = [cross(0, 1)], []
    rows = pl.ds(pl.multiple_of(c * 256, 256), 256)
    feats = [
        go(feat_ref.at[rows], fall.at[0, 2], yp),
        go(feat_ref.at[rows], fall.at[0, 0], ym),
        go(feat_ref.at[rows], fall.at[0, 1], y2),
    ]
    for copy in first:
        copy.wait_recv()
    r0 = ring0(0)
    shared.append(share(0, 0, 1))
    for s in range(8):
        for copy in r1:
            copy.wait_recv()
        if s < 7:
            r1 = ring1(s + 1)
        for copy in r0:
            copy.wait_recv()
        if s < 7:
            r0 = ring0(s + 1)
        for group in crossed:
            cross_off(group)
        crossed = [cross_on(group) for group in crossing]
        crossing = []
        if s % 2 == 1:
            for lo, n in ((s, 2), (15 - s, 2)) if s < 7 else ((7, 2), (9, 1)):
                crossing.append(cross(lo, n))
                shared.append(share(0, lo, n))
        if s == 6:
            for copy in feats:
                copy.wait_recv()
            shared.append(go(fall.at[0], fall.at[1], sib))
    for group in crossed:
        cross_off(group)
    for group in crossing:
        cross_off(cross_on(group))
    for copy in shared:
        copy.wait_recv()
    go.finish()


def tile_kernel(item_at, context_at, user_at, tab, contexts, keys, users, values, profile, features, out):
    for i in range(SLAB // 256):
        rows = pl.ds(i * 256, 256)
        out[rows, :] = jnp.dot(profile[rows, :], features[...], preferred_element_type=F32)
    lane128 = lax.broadcasted_iota(jnp.int32, (TR, CB), 1)
    lane16 = lax.broadcasted_iota(jnp.int32, (TR, IB), 1)
    sub16 = lax.broadcasted_iota(jnp.int32, (UB, TR), 0)
    group = 8

    def step(g, carry):
        key = keys[g]
        user = users[pl.ds(pl.multiple_of(g * group, group), group), :]
        value = values[pl.ds(pl.multiple_of(g * group, group), group), :]
        sums = []
        for t in range(group):
            k = key[:, t : t + 1]
            context_onehot = (lax.shift_right_logical(jnp.broadcast_to(k, (TR, CB)), 4) == lane128).astype(F32).astype(BF16)
            item_onehot = (jnp.bitwise_and(jnp.broadcast_to(k, (TR, IB)), 15) == lane16).astype(F32).astype(BF16)
            at = g * group + t
            context_rows = contexts[pl.ds(pl.multiple_of(context_at[at], CB), CB), :]
            item_rows = tab[pl.ds(pl.multiple_of(item_at[at], IB), IB), :]
            product = jnp.dot(context_onehot, context_rows, preferred_element_type=F32) * jnp.dot(
                item_onehot, item_rows, preferred_element_type=F32
            )
            high = product.astype(BF16)
            low = (product - high.astype(F32)).astype(BF16)
            weight = jnp.where(user[t : t + 1, :] == sub16, value[t : t + 1, :], 0.0).astype(BF16)
            sums.append(
                jnp.dot(weight, high, preferred_element_type=F32) + jnp.dot(weight, low, preferred_element_type=F32)
            )
        for t in range(group):
            rows = pl.ds(pl.multiple_of(user_at[g * group + t], UB), UB)
            out[rows, :] += sums[t]
        return carry

    lax.fori_loop(0, TILES // group, step, 0)


def inverse(a, size=R, panel=32):
    lane = lax.broadcasted_iota(jnp.int32, (panel, size), 1)
    sub = lax.broadcasted_iota(jnp.int32, (panel, size), 0)
    wide = lax.broadcasted_iota(jnp.int32, (size, size), 1)
    for p in range(size // panel):
        lo = p * panel
        block = a[lo : lo + panel, :]
        for k in range(panel):
            at = lo + k
            column = jnp.broadcast_to(block[:, at : at + 1], (panel, size))
            pivot = 1.0 / jnp.broadcast_to(column[k : k + 1, :], (panel, size))
            row = jnp.where(lane == at, pivot, jnp.broadcast_to(block[k : k + 1, :], (panel, size)) * pivot)
            block = jnp.where(sub == k, row, jnp.where(lane == at, 0.0, block) - column * row)
        left = a[:, lo : lo + panel]
        a = jnp.where((wide >= lo) & (wide < lo + panel), 0.0, a) - jnp.dot(
            left, block, preferred_element_type=F32, precision=HIGHEST
        )
        pieces = [a[:lo, :]] if lo else []
        pieces.append(block)
        if lo + panel < size:
            pieces.append(a[lo + panel :, :])
        a = jnp.concatenate(pieces, axis=0)
    return a


def eye(size=R):
    return (
        lax.broadcasted_iota(jnp.int32, (size, size), 0) == lax.broadcasted_iota(jnp.int32, (size, size), 1)
    ).astype(F32)


def gram(a, b):
    return lax.dot_general(a, b, (((0,), (0,)), ((), ())), preferred_element_type=F32)


def normal_kernel(tab, contexts, features, fall, out):
    items = lax.fori_loop(
        0,
        8,
        lambda i, acc: acc + gram(tab[pl.ds(i * 1024, 1024), :], tab[pl.ds(i * 1024, 1024), :]),
        jnp.zeros((R, R), F32),
    )
    normal = items * gram(contexts[...], contexts[...]) + gram(features[...], features[...])
    normal = normal + gram(fall[...], fall[...]) + RIDGE * eye()
    out[...] = inverse(normal)


def user_kernel(part, inv, out, passing, landed, send_sem, recv_sem):
    y = position()[3]
    after, before = lax.rem(y + 1, NY), lax.rem(y + 3, NY)
    across = lax.rem(y + 2, NY)
    yp, ym = neighbour(dy=1), neighbour(dy=-1)
    top, low = pl.ds(0, 256), pl.ds(256, 256)
    greet([yp, ym])
    go = Sender(send_sem, recv_sem)
    ap = go(part.at[across, top], passing.at[0], yp)
    am = go(part.at[across, low], passing.at[1], ym)
    bp = go(part.at[after, low], landed.at[0], yp)
    bm = go(part.at[before, top], landed.at[1], ym)
    ap.wait_recv()
    passing[2] = passing[0] + part[after, top, :]
    cp = go(passing.at[2], landed.at[2], yp)
    am.wait_recv()
    passing[3] = passing[1] + part[before, low, :]
    cm = go(passing.at[3], landed.at[3], ym)
    bm.wait_recv()
    cp.wait_recv()
    total = part[y, top, :] + landed[1] + landed[2]
    out[y, top, :] = jnp.dot(total, inv[...], preferred_element_type=F32, precision=HIGHEST).astype(BF16)
    up0 = go(out.at[y, top], out.at[y, top], yp)
    um0 = go(out.at[y, top], out.at[y, top], ym)
    bp.wait_recv()
    cm.wait_recv()
    total = part[y, low, :] + landed[0] + landed[3]
    out[y, low, :] = jnp.dot(total, inv[...], preferred_element_type=F32, precision=HIGHEST).astype(BF16)
    up1 = go(out.at[y, low], out.at[y, low], yp)
    um1 = go(out.at[y, low], out.at[y, low], ym)
    up0.wait_recv()
    vp = go(out.at[before, top], out.at[before, top], yp)
    um1_wait = um1
    um0.wait_recv()
    um1_wait.wait_recv()
    vm = go(out.at[after, low], out.at[after, low], ym)
    up1.wait_recv()
    vp.wait_recv()
    vm.wait_recv()
    go.finish()


def reduce_kernel(uf, profile, outg, outf, pg, pf, cg, cf, sg, sf, xg, xf, tg, tf, zg, zf, send_sem, recv_sem):
    z, x, c, _ = position()
    sib = neighbour(dc=1)
    xs = [neighbour(dx=d) for d in range(1, NX)]
    zs = [neighbour(dz=d) for d in range(1, NZ)]
    whole = gram(uf[...], uf[...])
    pg[0] = whole[:, :128]
    pg[1] = whole[:, 128:]
    whole = gram(profile[...], uf[...])
    pf[0] = whole[:, :128]
    pf[1] = whole[:, 128:]
    greet([sib] + xs + zs)
    go = Sender(send_sem, recv_sem)
    other = lax.rem(c + 1, 2)
    kg = go(pg.at[other], cg, sib)
    kf = go(pf.at[other], cf, sib)

    def over_x(k, part, came, held, slots, rows):
        k.wait_recv()
        held[...] = (part[c] + came[...]).reshape(NX, rows, 128)
        return [go(held.at[lax.rem(x + d, NX)], slots.at[d - 1], xs[d - 1]) for d in range(1, NX)]

    ag = over_x(kg, pg, cg, sg, xg, 64)
    af = over_x(kf, pf, cf, sf, xf, 128)

    def over_z(copies, held, slots, split, zslots, rows):
        total = held[x]
        for d, copy in enumerate(copies):
            copy.wait_recv()
            total = total + slots[d]
        for i in range(NZ):
            split[i] = total[i * rows : (i + 1) * rows, :]
        return [go(split.at[lax.rem(z + d, NZ)], zslots.at[d - 1], zs[d - 1]) for d in range(1, NZ)]

    bg = over_z(ag, sg, xg, tg, zg, 4)
    bf = over_z(af, sf, xf, tf, zf, 8)

    def back_z(copies, split, zslots, out):
        total = split[z]
        for d, copy in enumerate(copies):
            copy.wait_recv()
            total = total + zslots[d]
        out[c, x, z] = total
        return [go(out.at[c, x, z], out.at[c, x, z], zs[d - 1]) for d in range(1, NZ)]

    hg = back_z(bg, tg, zg, outg)
    hf = back_z(bf, tf, zf, outf)

    def back_x(copies, out):
        for copy in copies:
            copy.wait_recv()
        return [go(out.at[c, x], out.at[c, x], xs[d - 1]) for d in range(1, NX)]

    ig = back_x(hg, outg)
    jf = back_x(hf, outf)

    def back_c(copies, out):
        for copy in copies:
            copy.wait_recv()
        return go(out.at[c], out.at[c], sib)

    lg = back_c(ig, outg)
    lf = back_c(jf, outf)
    lg.wait_recv()
    lf.wait_recv()
    go.finish()


def feature_kernel(gathered, right, out, normal):
    for h in range(2):
        for x in range(NX):
            for z in range(NZ):
                at = x * 64 + z * 4
                normal[at : at + 4, h * 128 : (h + 1) * 128] = gathered[h, x, z]
    inv = inverse(normal[...] + RIDGE * eye())
    total = jnp.dot(right[0], inv[:128, :], preferred_element_type=F32, precision=HIGHEST)
    total = total + jnp.dot(right[1], inv[128:, :], preferred_element_type=F32, precision=HIGHEST)
    out[...] = total.astype(BF16)


VM = pl.BlockSpec(memory_space=pltpu.VMEM)
SM = pl.BlockSpec(memory_space=pltpu.SMEM)


def remote_params(number):
    return pltpu.CompilerParams(collective_id=number, has_side_effects=True, vmem_limit_bytes=VMEM_LIMIT)


PLAIN = pltpu.CompilerParams(vmem_limit_bytes=VMEM_LIMIT)


def shape(dims, dtype):
    return jax.ShapeDtypeStruct(dims, dtype)


def sems(n):
    return [pltpu.SemaphoreType.DMA((n,)), pltpu.SemaphoreType.DMA((n,))]


def local(
    tile_users,
    tile_owners,
    tile_blocks,
    tile_contexts,
    row_users,
    row_items,
    row_contexts,
    tile_values,
    tile_count,
    item_factors,
    context_factors,
    profile,
    feature_factors,
):
    z, x, c, _ = position()
    owners = tile_owners.reshape(TILES)
    blocks = tile_blocks.reshape(TILES)
    rel_z = (owners // 8 - z) % NZ
    rel_x = (owners // 2 % 4 - x) % NX
    rel_c = (owners % 2 - c) % NC
    item_at = ((((blocks // 2) * 2 + rel_c) * NZ + rel_z) * NX + rel_x) * 32 + (blocks % 2) * IB
    context_at = tile_contexts.reshape(TILES) * CB
    user_at = tile_users.reshape(TILES) * UB
    keys = row_contexts.reshape(TILES, TR) * IB + row_items.reshape(TILES, TR)
    keys = keys.reshape(TILES // 8, 8, TR).transpose(0, 2, 1)
    alive = jnp.arange(TILES, dtype=jnp.int32) < tile_count.reshape(())
    values = jnp.where(alive[:, None], tile_values.reshape(TILES, TR).astype(F32), 0.0)
    users = row_users.reshape(TILES, TR)

    tab, fall = pl.pallas_call(
        gather_kernel,
        out_shape=(shape((2, 2, NZ, NX, 32, R), BF16), shape((2, 3, 256, R), BF16)),
        in_specs=[VM, VM],
        out_specs=(VM, VM),
        scratch_shapes=sems(96),
        compiler_params=remote_params(0),
        name="gather_items",
    )(item_factors, feature_factors)
    tab = tab.reshape(8192, R)
    fall = fall.reshape(1536, R)
    part = pl.pallas_call(
        tile_kernel,
        out_shape=shape((SLAB, R), F32),
        in_specs=[SM] * 3 + [VM] * 7,
        out_specs=VM,
        compiler_params=PLAIN,
        name="tiles",
    )(item_at, context_at, user_at, tab, context_factors, keys, users, values, profile, feature_factors)
    inv = pl.pallas_call(
        normal_kernel,
        out_shape=shape((R, R), F32),
        in_specs=[VM] * 4,
        out_specs=VM,
        compiler_params=PLAIN,
        name="normal_inverse",
    )(tab, context_factors, feature_factors, fall)
    uf = pl.pallas_call(
        user_kernel,
        out_shape=shape((NY, 512, R), BF16),
        in_specs=[VM, VM],
        out_specs=VM,
        scratch_shapes=[pltpu.VMEM((4, 256, R), F32), pltpu.VMEM((4, 256, R), F32)] + sems(12),
        compiler_params=remote_params(1),
        name="user_rows",
    )(part.reshape(NY, 512, R), inv)
    uf = uf.reshape(SLAB, R)
    gathered, right = pl.pallas_call(
        reduce_kernel,
        out_shape=(shape((2, NX, NZ, 4, 128), F32), shape((2, NX, NZ, 8, 128), F32)),
        in_specs=[VM, VM],
        out_specs=(VM, VM),
        scratch_shapes=[
            pltpu.VMEM((2, 256, 128), F32),
            pltpu.VMEM((2, 512, 128), F32),
            pltpu.VMEM((256, 128), F32),
            pltpu.VMEM((512, 128), F32),
            pltpu.VMEM((NX, 64, 128), F32),
            pltpu.VMEM((NX, 128, 128), F32),
            pltpu.VMEM((3, 64, 128), F32),
            pltpu.VMEM((3, 128, 128), F32),
            pltpu.VMEM((NZ, 4, 128), F32),
            pltpu.VMEM((NZ, 8, 128), F32),
            pltpu.VMEM((NZ - 1, 4, 128), F32),
            pltpu.VMEM((NZ - 1, 8, 128), F32),
        ]
        + sems(76),
        compiler_params=remote_params(2),
        name="sum_over_users",
    )(uf, profile)
    feature_new = pl.pallas_call(
        feature_kernel,
        out_shape=shape((512, R), BF16),
        in_specs=[VM, VM],
        out_specs=VM,
        scratch_shapes=[pltpu.VMEM((R, R), F32)],
        compiler_params=PLAIN,
        name="feature_rows",
    )(gathered, right.reshape(2, 512, 128))
    return (uf, feature_new)


def solution(mesh):
    in_specs = (
        P("users", "items", None),
        P("users", "items", None, None),
        P("users", "items", None),
        P("users", "items", None),
        P("users", "items", None, None),
        P("users", "items", None, None),
        P("users", "items", None, None),
        P("users", "items", None, None),
        P("users", "items"),
        P("users", None),
        P(),
        P("users", "items"),
        P("items", None),
    )
    out_specs = (P("users", None), P("items", None))
    return jax.shard_map(local, mesh=mesh, in_specs=in_specs, out_specs=out_specs, check_vma=False)
```

time: 979 us -> 264 us (0.27); the launches traced: 969 us -> 264 us
  waiting for transfers between devices: 697 us -> 0 us
  Pallas kernels: 0 us -> 256 us
  other arithmetic: 121 us -> 4.74 us
  matrix products: 48.9 us -> 0 us
  local copies, waits for them, and re-layouts: 40.7 us -> 2.29 us
  blocking collectives: 35.1 us -> 0 us
  between operations: 17.8 us -> 1.33 us
    psum x3 -> x0, waiting for transfers between devices: 602 us -> none  [the longest x1 330 us: local(): lax.psum((gram(user_factors), feature_terms), 'users')]
    pallas_call x0 -> x6, Pallas kernels: none -> 256 us  [the longest x1 65.6 us: local(): pl.pallas_call(gather_kernel, out_shape=(shape((2, 2, NZ, NX, 32, R), BF1...]
    another operation x18 -> x0, other arithmetic: 108 us -> none  [the longest x13 68.6 us: solve_rows(): cholesky_factor = jnp.linalg.cholesky(normal)]
    all_to_all x1 -> x0, waiting for transfers between devices: 95.1 us -> none  [local(): lax.all_to_all(answered, 'users', split_axis=0, concat_axis=0, tiled=True)]
    dot_general x22 -> x0, matrix products: 37.2 us -> none  [the longest x4 16 us: add_group(): jnp.einsum('bg,gur->bur', block_onehot, per_tile, precision=lax.Precision...]
    all_to_all x1 -> x0, blocking collectives: 35.1 us -> none  [local(): lax.all_to_all(wanted.reshape(users_size, capacity), 'users', split_axis=...]
    gather x9 -> x0, local copies, waits for them, and re-layouts: 18 us -> none  [the longest x4 8.6 us: add_group(): item_blocks = fetched[window(tile_place)]]
    another operation x16 -> x0, matrix products: 11.7 us -> none  [the longest x12 10.8 us: solve_rows(): return jax.scipy.linalg.cho_solve((cholesky_factor, True), right_side.T).T]
  transfers between devices with their start and end apart: 4 -> 0, of which waited for: 4 -> 0; matrix products, arithmetic and copies ran while one was open for 7% -> 0% of each run, Pallas kernels for 0% -> 0%
where the time goes in v1:
time: 264 us
  Pallas kernels  256 us (97%)
  other arithmetic  4.74 us (2%)
    pallas_call x1, Pallas kernels, local(): pl.pallas_call(gather_kernel, out_shape=(shape((2, 2, NZ, NX, 32, R), BF1...  65.6 us
    pallas_call x1, Pallas kernels, local(): pl.pallas_call(normal_kernel, out_shape=shape((R, R), F32), in_specs=[VM]...  43.5 us
    pallas_call x1, Pallas kernels, local(): pl.pallas_call(reduce_kernel, out_shape=(shape((2, NX, NZ, 4, 128), F32),...  43.3 us
    pallas_call x1, Pallas kernels, local(): pl.pallas_call(feature_kernel, out_shape=shape((512, R), BF16), in_specs=...  39.5 us
    pallas_call x1, Pallas kernels, local(): pl.pallas_call(user_kernel, out_shape=shape((NY, 512, R), BF16), in_specs...  33.2 us
    pallas_call x1, Pallas kernels, local(): pl.pallas_call(tile_kernel, out_shape=shape((SLAB, R), F32), in_specs=[SM...  30.4 us

profile of v1, /device:TPU:1, one launch (start us, length us, event | category | flops | bytes accessed | tf_op | source)
XLA Modules:
  0.0 264.0 jit_solution(2941289438933715710)
XLA Ops:
  1.3 1.2 fusion.6.item_at
  2.5 1.2 multiply_bitcast_fusion
  3.7 1.5 convert_select_fusion.values
  5.2 0.9 add_bitcast_fusion
  6.0 1.3 copy.15
  7.4 65.6 %gather_items.1 = (bf16[2,2,16,4,32,256]{5,4,3,2,1,0:T(8,128)(2,1)}, bf16[2,3,256,256]{3,2,1,0:T(8,128)(2,1)}) custom-call(bf16[64,256]{1,0:T(8,128)(2,1)} %item_ref.1, bf16[512,256]{1,0:T(8,128)(2,1)} %features.3), custom_call_target="tpu_custom_call" | custom-call | tf_op jit(solution)/shard_map/gather_items/pallas_call | solution.py:428
  73.0 43.5 %normal_inverse.1.inv = f32[256,256]{1,0:T(8,128)} custom-call(bf16[8192,256]{1,0:T(8,128)(2,1)} %bitcast.47, bf16[1024,256]{1,0:T(8,128)(2,1)} %contexts.3, bf16[512,256]{1,0:T(8,128)(2,1)} %features.3, bf16[1536,256]{1,0:T(8,128)(2,1)} %bitcast.53), custom_call_target="tpu_custom_call" | custom-call | tf_op jit(solution)/shard_map/normal_inverse/pallas_call | solution.py:447
  116.5 30.4 %tiles.1 = f32[2048,256]{1,0:T(8,128)} custom-call(s32[128]{0:T(128)} %fusion.6.item_at, s32[128]{0:T(128)} %get-tuple-element.11.context_at, s32[128]{0:T(128)} %get-tuple-element.10.user_at, bf16[8192,256]{1,0:T(8,128)(2,1)} %bitcast.48, bf16[1024,256]{1,0:T(8,128)(2,1)} %contexts.3, s32[16,128,8]{2,1,0:T(8,128)} %bitcast.52, s32[128,128]{1,0:T(8,128)} %bitcast.55, ...), custom_call_target="tpu_custom_call" | custom-call | tf_op jit(solution)/shard_map/tiles/pallas_call | solution.py:439
  146.9 33.2 %user_rows.1 = bf16[4,512,256]{2,1,0:T(8,128)(2,1)} custom-call(f32[4,512,256]{2,1,0:T(8,128)} %bitcast.51, f32[256,256]{1,0:T(8,128)} %normal_inverse.1.inv), custom_call_target="tpu_custom_call" | custom-call | tf_op jit(solution)/shard_map/user_rows/pallas_call | solution.py:455
  180.2 0.0 copy-start
  180.2 43.3 %sum_over_users.1 = (f32[2,4,16,4,128]{4,3,2,1,0:T(4,128)}, f32[2,4,16,8,128]{4,3,2,1,0:T(8,128)}) custom-call(bf16[2048,256]{1,0:T(8,128)(2,1)} %bitcast.49, bf16[2048,512]{1,0:T(8,128)(2,1)} %profile.3), custom_call_target="tpu_custom_call" | custom-call | tf_op jit(solution)/shard_map/sum_over_users/pallas_call | solution.py:465
  223.5 39.5 %feature_rows.1 = bf16[512,256]{1,0:T(8,128)(2,1)} custom-call(f32[2,4,16,4,128]{4,3,2,1,0:T(4,128)} %get-tuple-element.8.gathered, f32[2,512,128]{2,1,0:T(8,128)} %bitcast.54), custom_call_target="tpu_custom_call" | custom-call | tf_op jit(solution)/shard_map/feature_rows/pallas_call | solution.py:488
  263.0 0.0 copy-done
  263.0 1.0 copy.18
  (1 shorter events, 0.0 us)
Async XLA Ops:
  180.2 82.8 %copy-start = (bf16[4,512,256]{2,1,0:T(8,128)(2,1)S(1)}, bf16[4,512,256]{2,1,0:T(8,128)(2,1)}, u32[]{:S(2)}) copy-start(bf16[4,512,256]{2,1,0:T(8,128)(2,1)} %user_rows.1) | copy-start | bytes 3145732

commit v2 on v1

v2 whole, which is shorter than its diff:
```python
import functools

import jax
import jax.numpy as jnp
from jax import lax
from jax.experimental import pallas as pl
from jax.experimental.pallas import tpu as pltpu
from jax.sharding import PartitionSpec as P

NZ, NX, NC, NY = 16, 4, 2, 4
R = 256
CB, IB, UB, TR = 128, 16, 16, 128
TILES = 128
SLAB = 2048
RIDGE = 1.0
MESH = pl.DeviceIdType.MESH
F32 = jnp.float32
BF16 = jnp.bfloat16
HIGHEST = lax.Precision.HIGHEST
VMEM_LIMIT = 56 * 1024 * 1024


def position():
    u = lax.axis_index("users")
    y = lax.axis_index("items")
    return lax.div(u, 8), lax.rem(lax.div(u, 2), 4), lax.rem(u, 2), y


def neighbour(dz=0, dx=0, dc=0, dy=0):
    z, x, c, y = position()
    zz = lax.rem(z + dz + NZ, NZ)
    xx = lax.rem(x + dx + NX, NX)
    cc = lax.rem(c + dc, NC)
    return (zz * 8 + xx * 2 + cc, lax.rem(y + dy + NY, NY))


def greet(devices):
    barrier = pltpu.get_barrier_semaphore()
    for device in devices:
        pl.semaphore_signal(barrier, inc=1, device_id=device, device_id_type=MESH)
    pl.semaphore_wait(barrier, len(devices))


class Sender:
    def __init__(self, send_sem, recv_sem):
        self.send_sem, self.recv_sem, self.sent = send_sem, recv_sem, []

    def __call__(self, src, dst, device):
        i = len(self.sent)
        copy = pltpu.make_async_remote_copy(
            src_ref=src,
            dst_ref=dst,
            send_sem=self.send_sem.at[i],
            recv_sem=self.recv_sem.at[i],
            device_id=device,
            device_id_type=MESH,
        )
        copy.start()
        self.sent.append(copy)
        return copy

    def finish(self):
        for copy in self.sent:
            copy.wait_send()


def gather_kernel(item_ref, feat_ref, tab, fall, send_sem, recv_sem):
    c = position()[2]
    xp, xm, x2 = neighbour(dx=1), neighbour(dx=-1), neighbour(dx=2)
    zp, zm, sib = neighbour(dz=1), neighbour(dz=-1), neighbour(dc=1)
    yp, ym, y2 = neighbour(dy=1), neighbour(dy=-1), neighbour(dy=2)
    tab[0, 0, 0] = item_ref[...]
    greet([xp, xm, x2, zp, zm, sib, yp, ym, y2])
    go = Sender(send_sem, recv_sem)

    def up(s, e):
        return go(tab.at[0, (-s) % 16, e], tab.at[0, (-s - 1) % 16, e], zp)

    def down(s, e):
        return go(tab.at[0, s, e], tab.at[0, s + 1, e], zm)

    def share(d):
        return go(tab.at[0, d], tab.at[1, d], sib)

    own = tab.at[0, 0, 0]
    arrivals = {
        3: go(own, tab.at[0, 0, 3], xp),
        1: go(own, tab.at[0, 0, 1], xm),
        2: go(own, tab.at[0, 0, 2], x2),
    }
    ups, downs = {0: up(0, 0)}, {0: down(0, 0)}
    rows = pl.ds(pl.multiple_of(c * 256, 256), 256)
    feats = [
        go(feat_ref.at[rows], fall.at[0, 2], yp),
        go(feat_ref.at[rows], fall.at[0, 0], ym),
        go(feat_ref.at[rows], fall.at[0, 1], y2),
    ]
    order = (0, 3, 1, 2)
    for e in order[1:]:
        arrivals[e].wait_recv()
        ups[e], downs[e] = up(0, e), down(0, e)
    shared = [share(0)]
    for s in range(8):
        for e in order:
            if e in ups:
                ups.pop(e).wait_recv()
                if s < 6 or (s == 6 and e in (0, 3)):
                    ups[e] = up(s + 1, e)
            if e in downs:
                downs.pop(e).wait_recv()
                if s < 6 or (s == 6 and e in (1, 2)):
                    downs[e] = down(s + 1, e)
        shared.append(share(s + 1))
        if s < 7:
            shared.append(share(15 - s))
        if s == 5:
            for copy in feats:
                copy.wait_recv()
            shared.append(go(fall.at[0], fall.at[1], sib))
    for copy in shared:
        copy.wait_recv()
    go.finish()


def tile_kernel(
    owners, blocks, tile_contexts, tile_users, count, tab, contexts, row_contexts, row_items, row_users, values, profile, features, out
):
    z, x, c, _ = position()
    live = count[0]
    for i in range(SLAB // 256):
        rows = pl.ds(i * 256, 256)
        out[rows, :] = jnp.dot(profile[rows, :], features[...], preferred_element_type=F32)
    lane128 = lax.broadcasted_iota(jnp.int32, (TR, CB), 1)
    lane16 = lax.broadcasted_iota(jnp.int32, (TR, IB), 1)
    sub16 = lax.broadcasted_iota(jnp.int32, (UB, TR), 0)
    group = 16

    def item_row(at):
        owner = owners[at]
        rel_z = jnp.bitwise_and(lax.shift_right_logical(owner, 3) - z + NZ, NZ - 1)
        rel_x = jnp.bitwise_and(lax.shift_right_logical(owner, 1) - x + NX, NX - 1)
        rel_c = jnp.bitwise_and(owner + c, 1)
        return ((rel_c * NZ + rel_z) * NX + rel_x) * 64 + blocks[at] * IB

    def step(g, carry):
        rows = pl.ds(pl.multiple_of(g * group, group), group)
        key = jnp.transpose(row_contexts[rows, :] * IB + row_items[rows, :])
        user = row_users[rows, :]
        value = values[rows, :].astype(F32)
        sums = []
        for t in range(group):
            k = key[:, t : t + 1]
            context_onehot = (lax.shift_right_logical(jnp.broadcast_to(k, (TR, CB)), 4) == lane128).astype(F32).astype(BF16)
            item_onehot = (jnp.bitwise_and(jnp.broadcast_to(k, (TR, IB)), 15) == lane16).astype(F32).astype(BF16)
            at = g * group + t
            context_rows = contexts[pl.ds(pl.multiple_of(tile_contexts[at] * CB, CB), CB), :]
            item_rows = tab[pl.ds(pl.multiple_of(item_row(at), IB), IB), :]
            product = jnp.dot(context_onehot, context_rows, preferred_element_type=F32) * jnp.dot(
                item_onehot, item_rows, preferred_element_type=F32
            )
            high = product.astype(BF16)
            low = (product - high.astype(F32)).astype(BF16)
            weight = jnp.where((user[t : t + 1, :] == sub16) & (at < live), value[t : t + 1, :], 0.0).astype(BF16)
            sums.append(
                jnp.dot(weight, high, preferred_element_type=F32) + jnp.dot(weight, low, preferred_element_type=F32)
            )
        for t in range(group):
            place = pl.ds(pl.multiple_of(tile_users[g * group + t] * UB, UB), UB)
            out[place, :] += sums[t]
        return carry

    lax.fori_loop(0, TILES // group, step, 0)


def sweep(block, group):
    panel, size = block.shape
    lane = lax.broadcasted_iota(jnp.int32, (panel, size), 1)
    lane1 = lax.broadcasted_iota(jnp.int32, (1, size), 1)
    sub = lax.broadcasted_iota(jnp.int32, (panel, size), 0)
    sub1 = lax.broadcasted_iota(jnp.int32, (panel, 128), 0)

    def wide(v):
        return jnp.concatenate([v] * (size // 128), axis=1)

    for base in range(0, panel, group):
        columns = [jnp.broadcast_to(block[:, base + j : base + j + 1], (panel, 128)) for j in range(group)]
        for k in range(group):
            at = base + k
            pivot = 1.0 / columns[k][at : at + 1, :]
            row = jnp.where(lane1 == at, wide(pivot), block[at : at + 1, :] * wide(pivot))
            block = jnp.where(sub == at, row, jnp.where(lane == at, 0.0, block) - wide(columns[k]) * row)
            for j in range(k + 1, group):
                factor = columns[j][at : at + 1, :] * pivot
                columns[j] = jnp.where(sub1 == at, factor, columns[j] - columns[k] * factor)
    return block


def invert(ref, between=(), size=R, panel=32, group=16):
    hooks = dict(between)
    lane = lax.broadcasted_iota(jnp.int32, (size - panel, size), 1)

    def step(p, carry):
        block = sweep(ref[0:panel, :], group)
        rest = ref[panel:, :]
        update = jnp.dot(rest[:, 0:panel], block, preferred_element_type=F32, precision=HIGHEST)
        ref[0 : size - panel, :] = pltpu.roll(jnp.where(lane < panel, 0.0, rest) - update, size - panel, 1)
        ref[size - panel :, :] = pltpu.roll(block, size - panel, 1)
        return carry

    done = 0
    for p in sorted(set(hooks) | {size // panel - 1}):
        lax.fori_loop(done, p + 1, step, 0)
        done = p + 1
        if p in hooks:
            hooks[p]()


def eye(size=R):
    return (
        lax.broadcasted_iota(jnp.int32, (size, size), 0) == lax.broadcasted_iota(jnp.int32, (size, size), 1)
    ).astype(F32)


def gram(a, b):
    return lax.dot_general(a, b, (((0,), (0,)), ((), ())), preferred_element_type=F32)


def user_kernel(part, tab, contexts, features, fall, out, inv, passing, landed, send_sem, recv_sem):
    y = position()[3]
    after, before = lax.rem(y + 1, NY), lax.rem(y + 3, NY)
    across = lax.rem(y + 2, NY)
    yp, ym = neighbour(dy=1), neighbour(dy=-1)
    top, low = pl.ds(0, 256), pl.ds(256, 256)
    greet([yp, ym])
    go = Sender(send_sem, recv_sem)
    ap = go(part.at[across, top], passing.at[0], yp)
    am = go(part.at[across, low], passing.at[1], ym)
    bp = go(part.at[after, low], landed.at[0], yp)
    bm = go(part.at[before, top], landed.at[1], ym)
    items = lax.fori_loop(
        0,
        8,
        lambda i, acc: acc + gram(tab[pl.ds(i * 1024, 1024), :], tab[pl.ds(i * 1024, 1024), :]),
        jnp.zeros((R, R), F32),
    )
    normal = items * gram(contexts[...], contexts[...]) + gram(features[...], features[...])
    inv[...] = normal + gram(fall[...], fall[...]) + RIDGE * eye()
    ap.wait_recv()
    passing[2] = passing[0] + part[after, top, :]
    cp = go(passing.at[2], landed.at[2], yp)
    am.wait_recv()
    passing[3] = passing[1] + part[before, low, :]
    cm = go(passing.at[3], landed.at[3], ym)
    invert(inv)
    bm.wait_recv()
    cp.wait_recv()
    total = part[y, top, :] + landed[1] + landed[2]
    out[y, top, :] = jnp.dot(total, inv[...], preferred_element_type=F32, precision=HIGHEST).astype(BF16)
    up0 = go(out.at[y, top], out.at[y, top], yp)
    um0 = go(out.at[y, top], out.at[y, top], ym)
    bp.wait_recv()
    cm.wait_recv()
    total = part[y, low, :] + landed[0] + landed[3]
    out[y, low, :] = jnp.dot(total, inv[...], preferred_element_type=F32, precision=HIGHEST).astype(BF16)
    um1 = go(out.at[y, low], out.at[y, low], ym)
    up1 = go(out.at[y, low], out.at[y, low], yp)
    up0.wait_recv()
    vp = go(out.at[before, top], out.at[before, top], yp)
    um0.wait_recv()
    um1.wait_recv()
    vm = go(out.at[after, low], out.at[after, low], ym)
    up1.wait_recv()
    vp.wait_recv()
    vm.wait_recv()
    go.finish()


def reduce_kernel(uf, profile, out, normal, outg, outf, pg, pf, cg, cf, sg, sf, xg, xf, tg, tf, zg, zf, send_sem, recv_sem):
    z, x, c, _ = position()
    sib = neighbour(dc=1)
    xs = [neighbour(dx=d) for d in range(1, NX)]
    zs = [neighbour(dz=d) for d in range(1, NZ)]
    greet([sib] + xs + zs)
    go = Sender(send_sem, recv_sem)
    other = lax.rem(c + 1, 2)
    whole = gram(uf[...], uf[...])
    pg[0] = whole[:, :128]
    pg[1] = whole[:, 128:]
    kg = go(pg.at[other], cg, sib)
    whole = gram(profile[...], uf[...])
    pf[0] = whole[:, :128]
    pf[1] = whole[:, 128:]
    kf = go(pf.at[other], cf, sib)

    def over_x(k, part, came, held, slots, rows):
        k.wait_recv()
        held[...] = (part[c] + came[...]).reshape(NX, rows, 128)
        return [go(held.at[lax.rem(x + d, NX)], slots.at[d - 1], xs[d - 1]) for d in range(1, NX)]

    ag = over_x(kg, pg, cg, sg, xg, 64)

    def over_z(copies, held, slots, split, zslots, rows):
        total = held[x]
        for d, copy in enumerate(copies):
            copy.wait_recv()
            total = total + slots[d]
        for i in range(NZ):
            split[i] = total[i * rows : (i + 1) * rows, :]
        return [go(split.at[lax.rem(z + d, NZ)], zslots.at[d - 1], zs[d - 1]) for d in range(1, NZ)]

    bg = over_z(ag, sg, xg, tg, zg, 4)
    af = over_x(kf, pf, cf, sf, xf, 128)

    def back_z(copies, split, zslots, out):
        total = split[z]
        for d, copy in enumerate(copies):
            copy.wait_recv()
            total = total + zslots[d]
        out[c, x, z] = total
        return [go(out.at[c, x, z], out.at[c, x, z], zs[d - 1]) for d in range(1, NZ)]

    hg = back_z(bg, tg, zg, outg)

    def back_x(copies, out):
        for copy in copies:
            copy.wait_recv()
        return [go(out.at[c, x], out.at[c, x], xs[d - 1]) for d in range(1, NX)]

    ig = back_x(hg, outg)
    bf = over_z(af, sf, xf, tf, zf, 8)

    def back_c(copies, out):
        for copy in copies:
            copy.wait_recv()
        return go(out.at[c], out.at[c], sib)

    back_c(ig, outg).wait_recv()
    for half in range(2):
        for i in range(NX):
            for j in range(NZ):
                at = i * 64 + j * 4
                normal[at : at + 4, half * 128 : (half + 1) * 128] = outg[half, i, j]
    normal[...] += RIDGE * eye()
    later = {}

    def third():
        later["z"] = back_z(bf, tf, zf, outf)

    def fourth():
        later["x"] = back_x(later["z"], outf)

    def fifth():
        later["c"] = back_c(later["x"], outf)

    invert(normal, ((1, third), (3, fourth), (5, fifth)))
    later["c"].wait_recv()
    total = jnp.dot(outf[0].reshape(512, 128), normal[0:128, :], preferred_element_type=F32, precision=HIGHEST)
    total = total + jnp.dot(outf[1].reshape(512, 128), normal[128:, :], preferred_element_type=F32, precision=HIGHEST)
    out[...] = total.astype(BF16)
    go.finish()


VM = pl.BlockSpec(memory_space=pltpu.VMEM)
SM = pl.BlockSpec(memory_space=pltpu.SMEM)


def remote_params(number):
    return pltpu.CompilerParams(collective_id=number, has_side_effects=True, vmem_limit_bytes=VMEM_LIMIT)


PLAIN = pltpu.CompilerParams(vmem_limit_bytes=VMEM_LIMIT)


def shape(dims, dtype):
    return jax.ShapeDtypeStruct(dims, dtype)


def sems(n):
    return [pltpu.SemaphoreType.DMA((n,)), pltpu.SemaphoreType.DMA((n,))]


def local(
    tile_users,
    tile_owners,
    tile_blocks,
    tile_contexts,
    row_users,
    row_items,
    row_contexts,
    tile_values,
    tile_count,
    item_factors,
    context_factors,
    profile,
    feature_factors,
):
    tab, fall = pl.pallas_call(
        gather_kernel,
        out_shape=(shape((2, NZ, NX, 64, R), BF16), shape((2, 3, 256, R), BF16)),
        in_specs=[VM, VM],
        out_specs=(VM, VM),
        scratch_shapes=sems(96),
        compiler_params=remote_params(0),
        name="gather_items",
    )(item_factors, feature_factors)
    tab = tab.reshape(8192, R)
    fall = fall.reshape(1536, R)
    part = pl.pallas_call(
        tile_kernel,
        out_shape=shape((SLAB, R), F32),
        in_specs=[SM] * 5 + [VM] * 8,
        out_specs=VM,
        compiler_params=PLAIN,
        name="tiles",
    )(
        tile_owners.reshape(TILES),
        tile_blocks.reshape(TILES),
        tile_contexts.reshape(TILES),
        tile_users.reshape(TILES),
        tile_count.reshape(1),
        tab,
        context_factors,
        row_contexts.reshape(TILES, TR),
        row_items.reshape(TILES, TR),
        row_users.reshape(TILES, TR),
        tile_values.reshape(TILES, TR),
        profile,
        feature_factors,
    )
    uf = pl.pallas_call(
        user_kernel,
        out_shape=shape((NY, 512, R), BF16),
        in_specs=[VM] * 5,
        out_specs=VM,
        scratch_shapes=[
            pltpu.VMEM((R, R), F32),
            pltpu.VMEM((4, 256, R), F32),
            pltpu.VMEM((4, 256, R), F32),
        ]
        + sems(12),
        compiler_params=remote_params(1),
        name="user_rows",
    )(part.reshape(NY, 512, R), tab, context_factors, feature_factors, fall)
    uf = uf.reshape(SLAB, R)
    feature_new = pl.pallas_call(
        reduce_kernel,
        out_shape=shape((512, R), BF16),
        in_specs=[VM, VM],
        out_specs=VM,
        scratch_shapes=[
            pltpu.VMEM((R, R), F32),
            pltpu.VMEM((2, NX, NZ, 4, 128), F32),
            pltpu.VMEM((2, NX, NZ, 8, 128), F32),
            pltpu.VMEM((2, 256, 128), F32),
            pltpu.VMEM((2, 512, 128), F32),
            pltpu.VMEM((256, 128), F32),
            pltpu.VMEM((512, 128), F32),
            pltpu.VMEM((NX, 64, 128), F32),
            pltpu.VMEM((NX, 128, 128), F32),
            pltpu.VMEM((3, 64, 128), F32),
            pltpu.VMEM((3, 128, 128), F32),
            pltpu.VMEM((NZ, 4, 128), F32),
            pltpu.VMEM((NZ, 8, 128), F32),
            pltpu.VMEM((NZ - 1, 4, 128), F32),
            pltpu.VMEM((NZ - 1, 8, 128), F32),
        ]
        + sems(76),
        compiler_params=remote_params(2),
        name="feature_rows",
    )(uf, profile)
    return (uf, feature_new)


def solution(mesh):
    in_specs = (
        P("users", "items", None),
        P("users", "items", None, None),
        P("users", "items", None),
        P("users", "items", None),
        P("users", "items", None, None),
        P("users", "items", None, None),
        P("users", "items", None, None),
        P("users", "items", None, None),
        P("users", "items"),
        P("users", None),
        P(),
        P("users", "items"),
        P("items", None),
    )
    out_specs = (P("users", None), P("items", None))
    return jax.shard_map(local, mesh=mesh, in_specs=in_specs, out_specs=out_specs, check_vma=False)
```

time: 264 us -> 175 us (0.66)
  Pallas kernels: 256 us -> 171 us
  other arithmetic: 4.74 us -> 0 us
    pallas_call x4 -> x2, Pallas kernels: 192 us -> 106 us  [the longest x1 55.1 us: local(): pl.pallas_call(reduce_kernel, out_shape=shape((512, R), BF16), in_specs=[...]
where the time goes in v2:
time: 175 us; the launch traced here: 174 us
  Pallas kernels  171 us (98%)
  local copies, waits for them, and re-layouts  1.77 us (1%)
    pallas_call x1, Pallas kernels, local(): pl.pallas_call(reduce_kernel, out_shape=shape((512, R), BF16), in_specs=[...  55.1 us
    pallas_call x1, Pallas kernels, local(): pl.pallas_call(gather_kernel, out_shape=(shape((2, NZ, NX, 64, R), BF16),...  51.2 us
    pallas_call x1, Pallas kernels, local(): pl.pallas_call(user_kernel, out_shape=shape((NY, 512, R), BF16), in_specs...  34.9 us
    pallas_call x1, Pallas kernels, local(): pl.pallas_call(tile_kernel, out_shape=shape((SLAB, R), F32), in_specs=[SM...  29.4 us

profile of v2, /device:TPU:1, one launch (start us, length us, event | category | flops | bytes accessed | tf_op | source)
XLA Modules:
  0.0 173.7 jit_solution(12786305715948326728)
XLA Ops:
  1.3 51.2 %gather_items.1 = (bf16[2,16,4,64,256]{4,3,2,1,0:T(8,128)(2,1)}, bf16[2,3,256,256]{3,2,1,0:T(8,128)(2,1)}) custom-call(bf16[64,256]{1,0:T(8,128)(2,1)} %item_ref.1, bf16[512,256]{1,0:T(8,128)(2,1)} %features.3), custom_call_target="tpu_custom_call" | custom-call | tf_op jit(solution)/shard_map/gather_items/pallas_call | solution.py:397
  52.5 29.4 %tiles.1 = f32[2048,256]{1,0:T(8,128)} custom-call(s32[128]{0:T(128)} %bitcast.24, s32[128]{0:T(128)} %bitcast.25, s32[128]{0:T(128)} %bitcast.26, s32[128]{0:T(128)} %bitcast.27, s32[1]{0:T(128)} %bitcast.13.count, bf16[8192,256]{1,0:T(8,128)(2,1)} %bitcast.14, bf16[1024,256]{1,0:T(8,128)(2,1)} %contexts.3, s32[128,128]{1,0:T(8,128)} %bitcast.20, ...), custom_call_target="tpu_custom_call" | custom-call | tf_op jit(solution)/shard_map/tiles/pallas_call | solution.py:408
  81.9 34.9 %user_rows.1 = bf16[4,512,256]{2,1,0:T(8,128)(2,1)} custom-call(f32[4,512,256]{2,1,0:T(8,128)} %bitcast.18, bf16[8192,256]{1,0:T(8,128)(2,1)} %bitcast.15, bf16[1024,256]{1,0:T(8,128)(2,1)} %contexts.3, bf16[512,256]{1,0:T(8,128)(2,1)} %features.3, bf16[1536,256]{1,0:T(8,128)(2,1)} %bitcast.19), custom_call_target="tpu_custom_call" | custom-call | tf_op jit(solution)/shard_map/user_rows/pallas_call | solution.py:430
  116.7 0.0 copy-start
  116.7 55.1 %feature_rows.1 = bf16[512,256]{1,0:T(8,128)(2,1)} custom-call(bf16[2048,256]{1,0:T(8,128)(2,1)} %bitcast.16, bf16[2048,512]{1,0:T(8,128)(2,1)} %profile.3), custom_call_target="tpu_custom_call" | custom-call | tf_op jit(solution)/shard_map/feature_rows/pallas_call | solution.py:445
  171.9 0.0 copy-done
  171.9 0.0 copy-start.1
  171.9 1.0 copy.18
  172.9 0.1 copy-done.1
  173.0 0.7 copy.19
Async XLA Ops:
  116.7 55.2 %copy-start = (bf16[4,512,256]{2,1,0:T(8,128)(2,1)S(1)}, bf16[4,512,256]{2,1,0:T(8,128)(2,1)}, u32[]{:S(2)}) copy-start(bf16[4,512,256]{2,1,0:T(8,128)(2,1)} %user_rows.1) | copy-start | bytes 3145732
  171.9 1.1 copy-start.1

commit v3 on v2

--- a/solution.py
+++ b/solution.py
@@ -38,7 +38,7 @@
     barrier = pltpu.get_barrier_semaphore()
     for device in devices:
         pl.semaphore_signal(barrier, inc=1, device_id=device, device_id_type=MESH)
-    pl.semaphore_wait(barrier, len(devices))
+    return lambda: pl.semaphore_wait(barrier, len(devices))
 
 
 class Sender:
@@ -70,7 +70,7 @@
     zp, zm, sib = neighbour(dz=1), neighbour(dz=-1), neighbour(dc=1)
     yp, ym, y2 = neighbour(dy=1), neighbour(dy=-1), neighbour(dy=2)
     tab[0, 0, 0] = item_ref[...]
-    greet([xp, xm, x2, zp, zm, sib, yp, ym, y2])
+    greet([xp, xm, x2, zp, zm, sib, yp, ym, y2])()
     go = Sender(send_sem, recv_sem)
 
     def up(s, e):
@@ -122,8 +122,18 @@
     go.finish()
 
 
+def item_row(owner, block, z, x, c):
+    rel_z = jnp.bitwise_and(lax.shift_right_logical(owner, 3) - z + NZ, NZ - 1)
+    rel_x = jnp.bitwise_and(lax.shift_right_logical(owner, 1) - x + NX, NX - 1)
+    rel_c = jnp.bitwise_and(owner + c, 1)
+    return ((rel_c * NZ + rel_z) * NX + rel_x) * 64 + block * IB
+
+
+GROUP = 16
+
+
 def tile_kernel(
-    owners, blocks, tile_contexts, tile_users, count, tab, contexts, row_contexts, row_items, row_users, values, profile, features, out
+    owners, blocks, tile_contexts, tile_users, count, tab, contexts, row_contexts, row_items, row_users, values, profile, features, out, high, low
 ):
     z, x, c, _ = position()
     live = count[0]
@@ -133,43 +143,46 @@
     lane128 = lax.broadcasted_iota(jnp.int32, (TR, CB), 1)
     lane16 = lax.broadcasted_iota(jnp.int32, (TR, IB), 1)
     sub16 = lax.broadcasted_iota(jnp.int32, (UB, TR), 0)
-    group = 16
-
-    def item_row(at):
-        owner = owners[at]
-        rel_z = jnp.bitwise_and(lax.shift_right_logical(owner, 3) - z + NZ, NZ - 1)
-        rel_x = jnp.bitwise_and(lax.shift_right_logical(owner, 1) - x + NX, NX - 1)
-        rel_c = jnp.bitwise_and(owner + c, 1)
-        return ((rel_c * NZ + rel_z) * NX + rel_x) * 64 + blocks[at] * IB
-
-    def step(g, carry):
-        rows = pl.ds(pl.multiple_of(g * group, group), group)
+
+    def products(g, carry):
+        rows = pl.ds(pl.multiple_of(g * GROUP, GROUP), GROUP)
         key = jnp.transpose(row_contexts[rows, :] * IB + row_items[rows, :])
-        user = row_users[rows, :]
-        value = values[rows, :].astype(F32)
-        sums = []
-        for t in range(group):
+        for t in range(GROUP):
             k = key[:, t : t + 1]
             context_onehot = (lax.shift_right_logical(jnp.broadcast_to(k, (TR, CB)), 4) == lane128).astype(F32).astype(BF16)
             item_onehot = (jnp.bitwise_and(jnp.broadcast_to(k, (TR, IB)), 15) == lane16).astype(F32).astype(BF16)
-            at = g * group + t
+            at = g * GROUP + t
             context_rows = contexts[pl.ds(pl.multiple_of(tile_contexts[at] * CB, CB), CB), :]
-            item_rows = tab[pl.ds(pl.multiple_of(item_row(at), IB), IB), :]
+            item_rows = tab[pl.ds(pl.multiple_of(item_row(owners[at], blocks[at], z, x, c), IB), IB), :]
             product = jnp.dot(context_onehot, context_rows, preferred_element_type=F32) * jnp.dot(
                 item_onehot, item_rows, preferred_element_type=F32
             )
-            high = product.astype(BF16)
-            low = (product - high.astype(F32)).astype(BF16)
+            top = product.astype(BF16)
+            place = pl.ds(pl.multiple_of(at * TR, TR), TR)
+            high[place, :] = top
+            low[place, :] = (product - top.astype(F32)).astype(BF16)
+        return carry
+
+    def sums(g, carry):
+        rows = pl.ds(pl.multiple_of(g * GROUP, GROUP), GROUP)
+        user = row_users[rows, :]
+        value = values[rows, :].astype(F32)
+        done = []
+        for t in range(GROUP):
+            at = g * GROUP + t
             weight = jnp.where((user[t : t + 1, :] == sub16) & (at < live), value[t : t + 1, :], 0.0).astype(BF16)
-            sums.append(
-                jnp.dot(weight, high, preferred_element_type=F32) + jnp.dot(weight, low, preferred_element_type=F32)
+            place = pl.ds(pl.multiple_of(at * TR, TR), TR)
+            done.append(
+                jnp.dot(weight, high[place, :], preferred_element_type=F32)
+                + jnp.dot(weight, low[place, :], preferred_element_type=F32)
             )
-        for t in range(group):
-            place = pl.ds(pl.multiple_of(tile_users[g * group + t] * UB, UB), UB)
-            out[place, :] += sums[t]
+        for t in range(GROUP):
+            place = pl.ds(pl.multiple_of(tile_users[g * GROUP + t] * UB, UB), UB)
+            out[place, :] += done[t]
         return carry
 
-    lax.fori_loop(0, TILES // group, step, 0)
+    lax.fori_loop(0, TILES // GROUP, products, 0)
+    lax.fori_loop(0, TILES // GROUP, sums, 0)
 
 
 def sweep(block, group):
@@ -225,18 +238,19 @@
     return lax.dot_general(a, b, (((0,), (0,)), ((), ())), preferred_element_type=F32)
 
 
-def user_kernel(part, tab, contexts, features, fall, out, inv, passing, landed, send_sem, recv_sem):
-    y = position()[3]
-    after, before = lax.rem(y + 1, NY), lax.rem(y + 3, NY)
-    across = lax.rem(y + 2, NY)
-    yp, ym = neighbour(dy=1), neighbour(dy=-1)
+def factor_kernel(
+    part, tab, contexts, features, fall, profile, out, new,
+    inv, passing, landed, outg, outf, pg, pf, cg, cf, sg, sf, xg, xf, tg, tf, zg, zf, yg, send_sem, recv_sem,
+):
+    z, x, c, y = position()
+    after, before, across = lax.rem(y + 1, NY), lax.rem(y + 3, NY), lax.rem(y + 2, NY)
+    yp, ym, y2 = neighbour(dy=1), neighbour(dy=-1), neighbour(dy=2)
+    sib = neighbour(dc=1)
+    xs = [neighbour(dx=d) for d in range(1, NX)]
+    zs = [neighbour(dz=d) for d in range(1, NZ)]
+    other = lax.rem(c + 1, 2)
     top, low = pl.ds(0, 256), pl.ds(256, 256)
-    greet([yp, ym])
-    go = Sender(send_sem, recv_sem)
-    ap = go(part.at[across, top], passing.at[0], yp)
-    am = go(part.at[across, low], passing.at[1], ym)
-    bp = go(part.at[after, low], landed.at[0], yp)
-    bm = go(part.at[before, top], landed.at[1], ym)
+    barrier = greet([yp, ym, y2, sib] + xs + zs)
     items = lax.fori_loop(
         0,
         8,
@@ -245,59 +259,40 @@
     )
     normal = items * gram(contexts[...], contexts[...]) + gram(features[...], features[...])
     inv[...] = normal + gram(fall[...], fall[...]) + RIDGE * eye()
-    ap.wait_recv()
-    passing[2] = passing[0] + part[after, top, :]
-    cp = go(passing.at[2], landed.at[2], yp)
-    am.wait_recv()
-    passing[3] = passing[1] + part[before, low, :]
-    cm = go(passing.at[3], landed.at[3], ym)
-    invert(inv)
+    barrier()
+    go = Sender(send_sem, recv_sem)
+
+    def relay_up():
+        ap.wait_recv()
+        passing[2] = passing[0] + part[after, top, :]
+        later["cp"] = go(passing.at[2], landed.at[2], yp)
+        am.wait_recv()
+        passing[3] = passing[1] + part[before, low, :]
+        later["cm"] = go(passing.at[3], landed.at[3], ym)
+
+    later = {}
+    ap = go(part.at[across, top], passing.at[0], yp)
+    am = go(part.at[across, low], passing.at[1], ym)
+    bp = go(part.at[after, low], landed.at[0], yp)
+    bm = go(part.at[before, top], landed.at[1], ym)
+    invert(inv, ((3, relay_up),))
     bm.wait_recv()
-    cp.wait_recv()
+    later["cp"].wait_recv()
     total = part[y, top, :] + landed[1] + landed[2]
     out[y, top, :] = jnp.dot(total, inv[...], preferred_element_type=F32, precision=HIGHEST).astype(BF16)
     up0 = go(out.at[y, top], out.at[y, top], yp)
     um0 = go(out.at[y, top], out.at[y, top], ym)
     bp.wait_recv()
-    cm.wait_recv()
+    later["cm"].wait_recv()
     total = part[y, low, :] + landed[0] + landed[3]
     out[y, low, :] = jnp.dot(total, inv[...], preferred_element_type=F32, precision=HIGHEST).astype(BF16)
     um1 = go(out.at[y, low], out.at[y, low], ym)
     up1 = go(out.at[y, low], out.at[y, low], yp)
-    up0.wait_recv()
-    vp = go(out.at[before, top], out.at[before, top], yp)
-    um0.wait_recv()
-    um1.wait_recv()
-    vm = go(out.at[after, low], out.at[after, low], ym)
-    up1.wait_recv()
-    vp.wait_recv()
-    vm.wait_recv()
-    go.finish()
-
-
-def reduce_kernel(uf, profile, out, normal, outg, outf, pg, pf, cg, cf, sg, sf, xg, xf, tg, tf, zg, zf, send_sem, recv_sem):
-    z, x, c, _ = position()
-    sib = neighbour(dc=1)
-    xs = [neighbour(dx=d) for d in range(1, NX)]
-    zs = [neighbour(dz=d) for d in range(1, NZ)]
-    greet([sib] + xs + zs)
-    go = Sender(send_sem, recv_sem)
-    other = lax.rem(c + 1, 2)
-    whole = gram(uf[...], uf[...])
-    pg[0] = whole[:, :128]
-    pg[1] = whole[:, 128:]
-    kg = go(pg.at[other], cg, sib)
-    whole = gram(profile[...], uf[...])
-    pf[0] = whole[:, :128]
-    pf[1] = whole[:, 128:]
-    kf = go(pf.at[other], cf, sib)
 
     def over_x(k, part, came, held, slots, rows):
         k.wait_recv()
         held[...] = (part[c] + came[...]).reshape(NX, rows, 128)
         return [go(held.at[lax.rem(x + d, NX)], slots.at[d - 1], xs[d - 1]) for d in range(1, NX)]
-
-    ag = over_x(kg, pg, cg, sg, xg, 64)
 
     def over_z(copies, held, slots, split, zslots, rows):
         total = held[x]
@@ -308,43 +303,64 @@
             split[i] = total[i * rows : (i + 1) * rows, :]
         return [go(split.at[lax.rem(z + d, NZ)], zslots.at[d - 1], zs[d - 1]) for d in range(1, NZ)]
 
-    bg = over_z(ag, sg, xg, tg, zg, 4)
-    af = over_x(kf, pf, cf, sf, xf, 128)
-
-    def back_z(copies, split, zslots, out):
+    def sum_z(copies, split, zslots):
         total = split[z]
         for d, copy in enumerate(copies):
             copy.wait_recv()
             total = total + zslots[d]
-        out[c, x, z] = total
-        return [go(out.at[c, x, z], out.at[c, x, z], zs[d - 1]) for d in range(1, NZ)]
-
-    hg = back_z(bg, tg, zg, outg)
-
-    def back_x(copies, out):
+        return total
+
+    def back_z(total, place):
+        place[c, x, z] = total
+        return [go(place.at[c, x, z], place.at[c, x, z], zs[d - 1]) for d in range(1, NZ)]
+
+    def back_x(copies, place):
         for copy in copies:
             copy.wait_recv()
-        return [go(out.at[c, x], out.at[c, x], xs[d - 1]) for d in range(1, NX)]
-
+        return [go(place.at[c, x], place.at[c, x], xs[d - 1]) for d in range(1, NX)]
+
+    def back_c(copies, place):
+        for copy in copies:
+            copy.wait_recv()
+        return go(place.at[c], place.at[c], sib)
+
+    whole = gram(out[y], out[y])
+    pg[0] = whole[:, :128]
+    pg[1] = whole[:, 128:]
+    kg = go(pg.at[other], cg, sib)
+    ag = over_x(kg, pg, cg, sg, xg, 64)
+    up0.wait_recv()
+    vp = go(out.at[before, top], out.at[before, top], yp)
+    bg = over_z(ag, sg, xg, tg, zg, 4)
+    um0.wait_recv()
+    um1.wait_recv()
+    vm = go(out.at[after, low], out.at[after, low], ym)
+    yg[0] = sum_z(bg, tg, zg)
+    hy = [go(yg.at[0], yg.at[1], yp), go(yg.at[0], yg.at[2], ym), go(yg.at[0], yg.at[3], y2)]
+    up1.wait_recv()
+    vp.wait_recv()
+    vm.wait_recv()
+    rows = out[...].reshape(SLAB, R)
+    whole = gram(profile[...], rows)
+    pf[0] = whole[:, :128]
+    pf[1] = whole[:, 128:]
+    kf = go(pf.at[other], cf, sib)
+    for copy in hy:
+        copy.wait_recv()
+    hg = back_z((yg[0] + yg[3]) + (yg[1] + yg[2]), outg)
+    af = over_x(kf, pf, cf, sf, xf, 128)
     ig = back_x(hg, outg)
     bf = over_z(af, sf, xf, tf, zf, 8)
-
-    def back_c(copies, out):
-        for copy in copies:
-            copy.wait_recv()
-        return go(out.at[c], out.at[c], sib)
-
     back_c(ig, outg).wait_recv()
     for half in range(2):
         for i in range(NX):
             for j in range(NZ):
                 at = i * 64 + j * 4
-                normal[at : at + 4, half * 128 : (half + 1) * 128] = outg[half, i, j]
-    normal[...] += RIDGE * eye()
-    later = {}
+                inv[at : at + 4, half * 128 : (half + 1) * 128] = outg[half, i, j]
+    inv[...] += RIDGE * eye()
 
     def third():
-        later["z"] = back_z(bf, tf, zf, outf)
+        later["z"] = back_z(sum_z(bf, tf, zf), outf)
 
     def fourth():
         later["x"] = back_x(later["z"], outf)
@@ -352,11 +368,11 @@
     def fifth():
         later["c"] = back_c(later["x"], outf)
 
-    invert(normal, ((1, third), (3, fourth), (5, fifth)))
+    invert(inv, ((1, third), (4, fourth), (6, fifth)))
     later["c"].wait_recv()
-    total = jnp.dot(outf[0].reshape(512, 128), normal[0:128, :], preferred_element_type=F32, precision=HIGHEST)
-    total = total + jnp.dot(outf[1].reshape(512, 128), normal[128:, :], preferred_element_type=F32, precision=HIGHEST)
-    out[...] = total.astype(BF16)
+    total = jnp.dot(outf[0].reshape(512, 128), inv[0:128, :], preferred_element_type=F32, precision=HIGHEST)
+    total = total + jnp.dot(outf[1].reshape(512, 128), inv[128:, :], preferred_element_type=F32, precision=HIGHEST)
+    new[...] = total.astype(BF16)
     go.finish()
 
 
@@ -410,6 +426,7 @@
         out_shape=shape((SLAB, R), F32),
         in_specs=[SM] * 5 + [VM] * 8,
         out_specs=VM,
+        scratch_shapes=[pltpu.VMEM((TILES * TR, R), BF16), pltpu.VMEM((TILES * TR, R), BF16)],
         compiler_params=PLAIN,
         name="tiles",
     )(
@@ -427,28 +444,15 @@
         profile,
         feature_factors,
     )
-    uf = pl.pallas_call(
-        user_kernel,
-        out_shape=shape((NY, 512, R), BF16),
-        in_specs=[VM] * 5,
-        out_specs=VM,
+    uf, feature_new = pl.pallas_call(
+        factor_kernel,
+        out_shape=(shape((NY, 512, R), BF16), shape((512, R), BF16)),
+        in_specs=[VM] * 6,
+        out_specs=(VM, VM),
         scratch_shapes=[
             pltpu.VMEM((R, R), F32),
             pltpu.VMEM((4, 256, R), F32),
             pltpu.VMEM((4, 256, R), F32),
-        ]
-        + sems(12),
-        compiler_params=remote_params(1),
-        name="user_rows",
-    )(part.reshape(NY, 512, R), tab, context_factors, feature_factors, fall)
-    uf = uf.reshape(SLAB, R)
-    feature_new = pl.pallas_call(
-        reduce_kernel,
-        out_shape=shape((512, R), BF16),
-        in_specs=[VM, VM],
-        out_specs=VM,
-        scratch_shapes=[
-            pltpu.VMEM((R, R), F32),
             pltpu.VMEM((2, NX, NZ, 4, 128), F32),
             pltpu.VMEM((2, NX, NZ, 8, 128), F32),
             pltpu.VMEM((2, 256, 128), F32),
@@ -463,12 +467,13 @@
             pltpu.VMEM((NZ, 8, 128), F32),
             pltpu.VMEM((NZ - 1, 4, 128), F32),
             pltpu.VMEM((NZ - 1, 8, 128), F32),
+            pltpu.VMEM((4, 4, 128), F32),
         ]
-        + sems(76),
-        compiler_params=remote_params(2),
-        name="feature_rows",
-    )(uf, profile)
-    return (uf, feature_new)
+        + sems(92),
+        compiler_params=remote_params(1),
+        name="factors",
+    )(part.reshape(NY, 512, R), tab, context_factors, feature_factors, fall, profile)
+    return (uf.reshape(SLAB, R), feature_new)
 
 
 def solution(mesh):

time: 175 us -> 150 us (0.86)
  Pallas kernels: 171 us -> 145 us
    pallas_call x1, Pallas kernels: 29.4 us -> 15.1 us  [local(): pl.pallas_call(tile_kernel, out_shape=shape((SLAB, R), F32), in_specs=[SM...]
    pallas_call x2 -> x1, Pallas kernels: 90 us -> 78.9 us  [local(): pl.pallas_call(factor_kernel, out_shape=(shape((NY, 512, R), BF16), shape...]
where the time goes in v3:
time: 150 us; the launch traced here: 149 us
  Pallas kernels  145 us (97%)
  local copies, waits for them, and re-layouts  3.01 us (2%)
    pallas_call x1, Pallas kernels, local(): pl.pallas_call(factor_kernel, out_shape=(shape((NY, 512, R), BF16), shape...  78.9 us
    pallas_call x1, Pallas kernels, local(): pl.pallas_call(gather_kernel, out_shape=(shape((2, NZ, NX, 64, R), BF16),...  51.2 us
    pallas_call x1, Pallas kernels, local(): pl.pallas_call(tile_kernel, out_shape=shape((SLAB, R), F32), in_specs=[SM...  15.1 us
    unnamed x4, local copies, waits for them, and re-layouts  3.01 us

profile of v3, /device:TPU:1, one launch (start us, length us, event | category | flops | bytes accessed | tf_op | source)
XLA Modules:
  0.0 149.5 jit_solution(15573743080674979147)
XLA Ops:
  1.3 51.2 %gather_items.1 = (bf16[2,16,4,64,256]{4,3,2,1,0:T(8,128)(2,1)}, bf16[2,3,256,256]{3,2,1,0:T(8,128)(2,1)}) custom-call(bf16[64,256]{1,0:T(8,128)(2,1)} %item_ref.1, bf16[512,256]{1,0:T(8,128)(2,1)} %features.3), custom_call_target="tpu_custom_call" | custom-call | tf_op jit(solution)/shard_map/gather_items/pallas_call | solution.py:413
  52.5 15.1 %tiles.1 = f32[2048,256]{1,0:T(8,128)} custom-call(s32[128]{0:T(128)} %bitcast.23, s32[128]{0:T(128)} %bitcast.24, s32[128]{0:T(128)} %bitcast.25, s32[128]{0:T(128)} %bitcast.26, s32[1]{0:T(128)} %bitcast.13.count, bf16[8192,256]{1,0:T(8,128)(2,1)} %bitcast.14, bf16[1024,256]{1,0:T(8,128)(2,1)} %contexts.3, s32[128,128]{1,0:T(8,128)} %bitcast.19, ...), custom_call_target="tpu_custom_call" | custom-call | tf_op jit(solution)/shard_map/tiles/pallas_call | solution.py:424
  67.6 78.9 %factors.1 = (bf16[4,512,256]{2,1,0:T(8,128)(2,1)}, bf16[512,256]{1,0:T(8,128)(2,1)}) custom-call(f32[4,512,256]{2,1,0:T(8,128)} %bitcast.16, bf16[8192,256]{1,0:T(8,128)(2,1)} %bitcast.15, bf16[1024,256]{1,0:T(8,128)(2,1)} %contexts.3, bf16[512,256]{1,0:T(8,128)(2,1)} %features.3, bf16[1536,256]{1,0:T(8,128)(2,1)} %bitcast.18, bf16[2048,512]{1,0:T(8,128)(2,1)} %profile.3), custom_call_target="tpu_custom_call" | custom-call | tf_op jit(solution)/shard_map/factors/pallas_call | solution.py:447
  146.5 0.0 copy-start
  146.5 2.3 %copy.18 = bf16[2048,256]{1,0:T(8,128)(2,1)} copy(bf16[2048,256]{1,0:T(8,128)(2,1)} %bitcast.17) | data formatting | bytes 2097152
  148.8 0.0 copy-done
  148.8 0.7 copy.19
Async XLA Ops:
  146.5 2.3 %copy-start = (bf16[512,256]{1,0:T(8,128)(2,1)S(1)}, bf16[512,256]{1,0:T(8,128)(2,1)}, u32[]{:S(2)}) copy-start(bf16[512,256]{1,0:T(8,128)(2,1)} %get-tuple-element.13) | copy-start | bytes 786436

commit v4 on v3

v4 whole, which is shorter than its diff:
```python
import functools

import jax
import jax.numpy as jnp
from jax import lax
from jax.experimental import pallas as pl
from jax.experimental.pallas import tpu as pltpu
from jax.sharding import PartitionSpec as P

NZ, NX, NC, NY = 16, 4, 2, 4
R = 256
CB, IB, UB, TR = 128, 16, 16, 128
TILES = 128
SLAB = 2048
RIDGE = 1.0
MESH = pl.DeviceIdType.MESH
F32 = jnp.float32
BF16 = jnp.bfloat16
HIGHEST = lax.Precision.HIGHEST
VMEM_LIMIT = 56 * 1024 * 1024


def position():
    u = lax.axis_index("users")
    y = lax.axis_index("items")
    return lax.div(u, 8), lax.rem(lax.div(u, 2), 4), lax.rem(u, 2), y


def neighbour(dz=0, dx=0, dc=0, dy=0):
    z, x, c, y = position()
    zz = lax.rem(z + dz + NZ, NZ)
    xx = lax.rem(x + dx + NX, NX)
    cc = lax.rem(c + dc, NC)
    return (zz * 8 + xx * 2 + cc, lax.rem(y + dy + NY, NY))


def greet(devices):
    barrier = pltpu.get_barrier_semaphore()
    for device in devices:
        pl.semaphore_signal(barrier, inc=1, device_id=device, device_id_type=MESH)
    return lambda: pl.semaphore_wait(barrier, len(devices))


class Sender:
    def __init__(self, send_sem, recv_sem):
        self.send_sem, self.recv_sem, self.sent = send_sem, recv_sem, []

    def __call__(self, src, dst, device):
        i = len(self.sent)
        copy = pltpu.make_async_remote_copy(
            src_ref=src,
            dst_ref=dst,
            send_sem=self.send_sem.at[i],
            recv_sem=self.recv_sem.at[i],
            device_id=device,
            device_id_type=MESH,
        )
        copy.start()
        self.sent.append(copy)
        return copy

    def finish(self):
        for copy in self.sent:
            copy.wait_send()


def item_place(owner, block, z, x, c):
    rel_z = jnp.bitwise_and(lax.shift_right_logical(owner, 3) - z + NZ, NZ - 1)
    rel_x = jnp.bitwise_and(lax.shift_right_logical(owner, 1) - x + NX, NX - 1)
    rel_c = jnp.bitwise_and(owner + c, 1)
    return ((rel_c * NZ + rel_z) * NX + rel_x) * 4 + block


GROUP = 16


def sweep(block, group):
    panel, size = block.shape
    lane = lax.broadcasted_iota(jnp.int32, (panel, size), 1)
    lane1 = lax.broadcasted_iota(jnp.int32, (1, size), 1)
    sub = lax.broadcasted_iota(jnp.int32, (panel, size), 0)
    sub1 = lax.broadcasted_iota(jnp.int32, (panel, 128), 0)

    def wide(v):
        return jnp.concatenate([v] * (size // 128), axis=1)

    for base in range(0, panel, group):
        columns = [jnp.broadcast_to(block[:, base + j : base + j + 1], (panel, 128)) for j in range(group)]
        for k in range(group):
            at = base + k
            pivot = 1.0 / columns[k][at : at + 1, :]
            row = jnp.where(lane1 == at, wide(pivot), block[at : at + 1, :] * wide(pivot))
            block = jnp.where(sub == at, row, jnp.where(lane == at, 0.0, block) - wide(columns[k]) * row)
            for j in range(k + 1, group):
                factor = columns[j][at : at + 1, :] * pivot
                columns[j] = jnp.where(sub1 == at, factor, columns[j] - columns[k] * factor)
    return block


def invert(ref, between=(), size=R, panel=32, group=16):
    hooks = dict(between)
    lane = lax.broadcasted_iota(jnp.int32, (size - panel, size), 1)

    def step(p, carry):
        block = sweep(ref[0:panel, :], group)
        rest = ref[panel:, :]
        update = jnp.dot(rest[:, 0:panel], block, preferred_element_type=F32, precision=HIGHEST)
        ref[0 : size - panel, :] = pltpu.roll(jnp.where(lane < panel, 0.0, rest) - update, size - panel, 1)
        ref[size - panel :, :] = pltpu.roll(block, size - panel, 1)
        return carry

    done = 0
    for p in sorted(set(hooks) | {size // panel - 1}):
        lax.fori_loop(done, p + 1, step, 0)
        done = p + 1
        if p in hooks:
            hooks[p]()


def eye(size=R):
    return (
        lax.broadcasted_iota(jnp.int32, (size, size), 0) == lax.broadcasted_iota(jnp.int32, (size, size), 1)
    ).astype(F32)


def gram(a, b):
    return lax.dot_general(a, b, (((0,), (0,)), ((), ())), preferred_element_type=F32)


def whole_kernel(
    owners, blocks, tile_contexts, count, item_ref, contexts, row_contexts, row_items, row_users, tile_users, values, profile, features,
    out, new,
    tab, fall, high, low, across_profile, part, sums,
    inv, passing, landed, outg, outf, pg, pf, cg, cf, sg, sf, xg, xf, tg, tf, zg, zf, yg, send_sem, recv_sem,
):
    z, x, c, y = position()
    yp, ym, y2 = neighbour(dy=1), neighbour(dy=-1), neighbour(dy=2)
    zp, zm, sib = neighbour(dz=1), neighbour(dz=-1), neighbour(dc=1)
    xs = [neighbour(dx=d) for d in range(1, NX)]
    zs = [neighbour(dz=d) for d in range(1, NZ)]
    other = lax.rem(c + 1, 2)
    barrier = greet([yp, ym, y2, sib] + xs + zs)
    go = Sender(send_sem, recv_sem)
    later = {}
    tab[0:4] = item_ref[...]

    def own_part(i, carry):
        rows = pl.ds(pl.multiple_of(i * 256, 256), 256)
        product = jnp.dot(profile[rows, :], features[...], preferred_element_type=F32)
        part[0, rows, :] = product[:, :128]
        part[1, rows, :] = product[:, 128:]
        return carry

    lane128 = lax.broadcasted_iota(jnp.int32, (TR, CB), 1)
    lane16 = lax.broadcasted_iota(jnp.int32, (TR, IB), 1)
    sub16 = lax.broadcasted_iota(jnp.int32, (UB, TR), 0)

    def group_rows(g):
        return pl.ds(pl.multiple_of(g * GROUP, GROUP), GROUP)

    def tile_rows(at):
        return pl.ds(pl.multiple_of(at * TR, TR), TR)

    def context_rows(g, carry):
        key = jnp.transpose(row_contexts[group_rows(g), :])
        for t in range(GROUP):
            onehot = (jnp.broadcast_to(key[:, t : t + 1], (TR, CB)) == lane128).astype(F32).astype(BF16)
            at = g * GROUP + t
            block = contexts[tile_contexts[at]]
            high[tile_rows(at), :] = jnp.dot(onehot, block, preferred_element_type=F32).astype(BF16)
        return carry

    def turn(i, carry):
        rows = pl.ds(pl.multiple_of(i * 256, 256), 256)
        across_profile[:, rows] = jnp.transpose(profile[rows, :])
        return carry

    def idle(fn, first, last):
        lax.fori_loop(first, last, fn, 0)

    idle(own_part, 0, 8)
    idle(context_rows, 0, 1)
    barrier()

    def place(core, d, e, n=1):
        return tab.at[pl.ds(((core * NZ + d) * NX + e) * 4, 4 * n)]

    def up(s, e):
        return go(place(0, (-s) % 16, e), place(0, (-s - 1) % 16, e), zp)

    def down(s, e):
        return go(place(0, s, e), place(0, s + 1, e), zm)

    def share(d):
        return go(place(0, d, 0, 4), place(1, d, 0, 4), sib)

    own = place(0, 0, 0)
    arrivals = {3: go(own, place(0, 0, 3), xs[0]), 1: go(own, place(0, 0, 1), xs[2]), 2: go(own, place(0, 0, 2), xs[1])}
    ups, downs = {0: up(0, 0)}, {0: down(0, 0)}
    rows = pl.ds(pl.multiple_of(c * 256, 256), 256)
    feats = [
        go(features.at[rows], fall.at[pl.ds(512, 256)], yp),
        go(features.at[rows], fall.at[pl.ds(0, 256)], ym),
        go(features.at[rows], fall.at[pl.ds(256, 256)], y2),
    ]
    order = (0, 3, 1, 2)
    for e in order[1:]:
        arrivals[e].wait_recv()
        ups[e], downs[e] = up(0, e), down(0, e)
    shared = [share(0)]
    for s in range(8):
        if s < 7:
            idle(context_rows, s + 1, s + 2)
        idle(turn, s, s + 1)
        for e in order:
            if e in ups:
                ups.pop(e).wait_recv()
                if s < 6 or (s == 6 and e in (0, 3)):
                    ups[e] = up(s + 1, e)
            if e in downs:
                downs.pop(e).wait_recv()
                if s < 6 or (s == 6 and e in (1, 2)):
                    downs[e] = down(s + 1, e)
        shared.append(share(s + 1))
        if s < 7:
            shared.append(share(15 - s))
        if s == 5:
            for copy in feats:
                copy.wait_recv()
            shared.append(go(fall.at[pl.ds(0, 768)], fall.at[pl.ds(768, 768)], sib))
    for copy in shared:
        copy.wait_recv()

    def products(g, carry):
        key = jnp.transpose(row_items[group_rows(g), :])
        for t in range(GROUP):
            onehot = (jnp.broadcast_to(key[:, t : t + 1], (TR, IB)) == lane16).astype(F32).astype(BF16)
            at = g * GROUP + t
            block = tab[item_place(owners[at], blocks[at], z, x, c)]
            product = jnp.dot(onehot, block, preferred_element_type=F32) * high[tile_rows(at), :].astype(F32)
            top = product.astype(BF16)
            high[tile_rows(at), :] = top
            low[tile_rows(at), :] = (product - top.astype(F32)).astype(BF16)
        return carry

    lax.fori_loop(0, TILES // GROUP, products, 0)
    live = jnp.broadcast_to(count[...], (GROUP, TR))
    order16 = lax.broadcasted_iota(jnp.int32, (GROUP, TR), 0)
    to_block = (lax.broadcasted_iota(jnp.int32, (128, TILES), 0) == jnp.broadcast_to(tile_users[...], (128, TILES))).astype(F32)
    to_block = jnp.concatenate([to_block.astype(BF16)] * 3, axis=1)
    after, before, across = lax.rem(y + 1, NY), lax.rem(y + 3, NY), lax.rem(y + 2, NY)

    def top(q):
        return pl.ds(pl.multiple_of(q * 512, 512), 256)

    def bottom(q):
        return pl.ds(pl.multiple_of(q * 512 + 256, 256), 256)

    def add_tiles(h):
        columns = slice(h * 128, h * 128 + 128)

        def tile_sums(g, carry):
            user = row_users[group_rows(g), :]
            value = jnp.where(order16 + g * GROUP < live, values[group_rows(g), :].astype(F32), 0.0)
            for t in range(GROUP):
                at = g * GROUP + t
                weight = jnp.where(user[t : t + 1, :] == sub16, value[t : t + 1, :], 0.0).astype(BF16)
                sums[group_rows(at), :] = jnp.dot(
                    weight, high[tile_rows(at), columns], preferred_element_type=F32
                ) + jnp.dot(weight, low[tile_rows(at), columns], preferred_element_type=F32)
            return carry

        lax.fori_loop(0, TILES // GROUP, tile_sums, 0)
        for u in range(UB):
            rows = pl.ds(u, 128, stride=UB)
            value = sums[rows, :]
            first = value.astype(BF16)
            value = value - first.astype(F32)
            second = value.astype(BF16)
            third = (value - second.astype(F32)).astype(BF16)
            total = jnp.dot(to_block, jnp.concatenate([first, second, third], axis=0), preferred_element_type=F32)
            sums[rows, :] = total
        part[h] += sums[...]
        ap = go(part.at[h, top(across)], passing.at[h, 0], yp)
        am = go(part.at[h, bottom(across)], passing.at[h, 1], ym)
        bp = go(part.at[h, bottom(after)], landed.at[h, 0], yp)
        bm = go(part.at[h, top(before)], landed.at[h, 1], ym)

        def relay():
            ap.wait_recv()
            passing[h, 2] = passing[h, 0] + part[h, top(after), :]
            cp = go(passing.at[h, 2], landed.at[h, 2], yp)
            am.wait_recv()
            passing[h, 3] = passing[h, 1] + part[h, bottom(before), :]
            cm = go(passing.at[h, 3], landed.at[h, 3], ym)
            later[h] = (bm, cp, bp, cm)

        return relay

    relays = [add_tiles(0), add_tiles(1)]
    def item_gram(i, acc):
        rows = tab[pl.ds(pl.multiple_of(i * 64, 64), 64)].reshape(1024, R)
        return acc + gram(rows, rows)

    items = lax.fori_loop(0, 8, item_gram, jnp.zeros((R, R), F32))
    table = contexts[...].reshape(1024, R)
    relays[0]()
    normal = items * gram(table, table) + gram(features[...], features[...])
    inv[...] = normal + gram(fall[...], fall[...]) + RIDGE * eye()
    invert(inv, ((1, relays[1]),))

    def solve(rows, copies, one, two):
        total = jnp.zeros((256, R), F32)
        for h in range(2):
            for i in copies:
                later[h][i].wait_recv()
            right = part[h, rows, :] + landed[h, one] + landed[h, two]
            total = total + jnp.dot(
                right, inv[h * 128 : h * 128 + 128, :], preferred_element_type=F32, precision=HIGHEST
            )
        out[rows, :] = total.astype(BF16)

    solve(top(y), (0, 1), 1, 2)
    up0 = go(out.at[top(y)], out.at[top(y)], yp)
    um0 = go(out.at[top(y)], out.at[top(y)], ym)
    solve(bottom(y), (2, 3), 0, 3)
    um1 = go(out.at[bottom(y)], out.at[bottom(y)], ym)
    up1 = go(out.at[bottom(y)], out.at[bottom(y)], yp)

    def over_x(k, part, came, held, slots, rows):
        k.wait_recv()
        held[...] = (part[c] + came[...]).reshape(NX, rows, 128)
        return [go(held.at[lax.rem(x + d, NX)], slots.at[d - 1], xs[d - 1]) for d in range(1, NX)]

    def over_z(copies, held, slots, split, zslots, rows):
        total = held[x]
        for d, copy in enumerate(copies):
            copy.wait_recv()
            total = total + slots[d]
        for i in range(NZ):
            split[i] = total[i * rows : (i + 1) * rows, :]
        return [go(split.at[lax.rem(z + d, NZ)], zslots.at[d - 1], zs[d - 1]) for d in range(1, NZ)]

    def sum_z(copies, split, zslots):
        total = split[z]
        for d, copy in enumerate(copies):
            copy.wait_recv()
            total = total + zslots[d]
        return total

    def back_z(total, place):
        place[c, x, z] = total
        return [go(place.at[c, x, z], place.at[c, x, z], zs[d - 1]) for d in range(1, NZ)]

    def back_x(copies, place):
        for copy in copies:
            copy.wait_recv()
        return [go(place.at[c, x], place.at[c, x], xs[d - 1]) for d in range(1, NX)]

    def back_c(copies, place):
        for copy in copies:
            copy.wait_recv()
        return go(place.at[c], place.at[c], sib)

    mine = out[pl.ds(pl.multiple_of(y * 512, 512), 512), :]
    whole = gram(mine, mine)
    pg[0] = whole[:, :128]
    pg[1] = whole[:, 128:]
    kg = go(pg.at[other], cg, sib)
    ag = over_x(kg, pg, cg, sg, xg, 64)
    up0.wait_recv()
    vp = go(out.at[top(before)], out.at[top(before)], yp)
    bg = over_z(ag, sg, xg, tg, zg, 4)
    um0.wait_recv()
    um1.wait_recv()
    vm = go(out.at[bottom(after)], out.at[bottom(after)], ym)
    yg[0] = sum_z(bg, tg, zg)
    hy = [go(yg.at[0], yg.at[1], yp), go(yg.at[0], yg.at[2], ym), go(yg.at[0], yg.at[3], y2)]
    up1.wait_recv()
    vp.wait_recv()
    vm.wait_recv()
    whole = jnp.dot(across_profile[...], out[...], preferred_element_type=F32)
    pf[0] = whole[:, :128]
    pf[1] = whole[:, 128:]
    kf = go(pf.at[other], cf, sib)
    for copy in hy:
        copy.wait_recv()
    hg = back_z((yg[0] + yg[3]) + (yg[1] + yg[2]), outg)
    af = over_x(kf, pf, cf, sf, xf, 128)
    ig = back_x(hg, outg)
    bf = over_z(af, sf, xf, tf, zf, 8)
    back_c(ig, outg).wait_recv()
    for half in range(2):
        for i in range(NX):
            for j in range(NZ):
                at = i * 64 + j * 4
                inv[at : at + 4, half * 128 : (half + 1) * 128] = outg[half, i, j]
    inv[...] += RIDGE * eye()

    def third():
        later["z"] = back_z(sum_z(bf, tf, zf), outf)

    def fourth():
        later["x"] = back_x(later["z"], outf)

    def fifth():
        later["c"] = back_c(later["x"], outf)

    invert(inv, ((1, third), (4, fourth), (6, fifth)))
    later["c"].wait_recv()
    total = jnp.dot(outf[0].reshape(512, 128), inv[0:128, :], preferred_element_type=F32, precision=HIGHEST)
    total = total + jnp.dot(outf[1].reshape(512, 128), inv[128:, :], preferred_element_type=F32, precision=HIGHEST)
    new[...] = total.astype(BF16)
    go.finish()


VM = pl.BlockSpec(memory_space=pltpu.VMEM)
SM = pl.BlockSpec(memory_space=pltpu.SMEM)


def remote_params(number):
    return pltpu.CompilerParams(collective_id=number, has_side_effects=True, vmem_limit_bytes=VMEM_LIMIT)


PLAIN = pltpu.CompilerParams(vmem_limit_bytes=VMEM_LIMIT)


def shape(dims, dtype):
    return jax.ShapeDtypeStruct(dims, dtype)


def sems(n):
    return [pltpu.SemaphoreType.DMA((n,)), pltpu.SemaphoreType.DMA((n,))]


def local(
    tile_users,
    tile_owners,
    tile_blocks,
    tile_contexts,
    row_users,
    row_items,
    row_contexts,
    tile_values,
    tile_count,
    item_factors,
    context_factors,
    profile,
    feature_factors,
):
    return tuple(
        pl.pallas_call(
            whole_kernel,
            out_shape=(shape((SLAB, R), BF16), shape((512, R), BF16)),
            in_specs=[SM] * 3 + [VM] * 10,
            out_specs=(VM, VM),
            scratch_shapes=[
                pltpu.VMEM((512, IB, R), BF16),
                pltpu.VMEM((1536, R), BF16),
                pltpu.VMEM((TILES * TR, R), BF16),
                pltpu.VMEM((TILES * TR, R), BF16),
                pltpu.VMEM((512, SLAB), BF16),
                pltpu.VMEM((2, SLAB, 128), F32),
                pltpu.VMEM((SLAB, 128), F32),
                pltpu.VMEM((R, R), F32),
                pltpu.VMEM((2, 4, 256, 128), F32),
                pltpu.VMEM((2, 4, 256, 128), F32),
                pltpu.VMEM((2, NX, NZ, 4, 128), F32),
                pltpu.VMEM((2, NX, NZ, 8, 128), F32),
                pltpu.VMEM((2, 256, 128), F32),
                pltpu.VMEM((2, 512, 128), F32),
                pltpu.VMEM((256, 128), F32),
                pltpu.VMEM((512, 128), F32),
                pltpu.VMEM((NX, 64, 128), F32),
                pltpu.VMEM((NX, 128, 128), F32),
                pltpu.VMEM((3, 64, 128), F32),
                pltpu.VMEM((3, 128, 128), F32),
                pltpu.VMEM((NZ, 4, 128), F32),
                pltpu.VMEM((NZ, 8, 128), F32),
                pltpu.VMEM((NZ - 1, 4, 128), F32),
                pltpu.VMEM((NZ - 1, 8, 128), F32),
                pltpu.VMEM((4, 4, 128), F32),
            ]
    + sems(200),
            compiler_params=remote_params(0),
            name="whole",
        )(
            tile_owners.reshape(TILES),
            tile_blocks.reshape(TILES),
            tile_contexts.reshape(TILES),
            tile_count,
            item_factors.reshape(4, IB, R),
            context_factors.reshape(8, CB, R),
            row_contexts.reshape(TILES, TR),
            row_items.reshape(TILES, TR),
            row_users.reshape(TILES, TR),
            tile_users.reshape(1, TILES),
            tile_values.reshape(TILES, TR),
            profile,
            feature_factors,
        )
    )


def solution(mesh):
    in_specs = (
        P("users", "items", None),
        P("users", "items", None, None),
        P("users", "items", None),
        P("users", "items", None),
        P("users", "items", None, None),
        P("users", "items", None, None),
        P("users", "items", None, None),
        P("users", "items", None, None),
        P("users", "items"),
        P("users", None),
        P(),
        P("users", "items"),
        P("items", None),
    )
    out_specs = (P("users", None), P("items", None))
    return jax.shard_map(local, mesh=mesh, in_specs=in_specs, out_specs=out_specs, check_vma=False)
```

time: 150 us -> 138 us (0.920)
  Pallas kernels: 145 us -> 134 us
    pallas_call x3 -> x1, Pallas kernels: 145 us -> 134 us  [local(): pl.pallas_call(whole_kernel, out_shape=(shape((SLAB, R), BF16), shape((51...]
where the time goes in v4:
time: 138 us
  Pallas kernels  134 us (97%)
  local copies, waits for them, and re-layouts  3.01 us (2%)
    pallas_call x1, Pallas kernels, local(): pl.pallas_call(whole_kernel, out_shape=(shape((SLAB, R), BF16), shape((51...  134 us
    unnamed x4, local copies, waits for them, and re-layouts  3.01 us

profile of v4, /device:TPU:1, one launch (start us, length us, event | category | flops | bytes accessed | tf_op | source)
XLA Modules:
  0.0 138.1 jit_solution(13855812977730147693)
XLA Ops:
  1.3 133.8 %whole.1 = (bf16[2048,256]{1,0:T(8,128)(2,1)}, bf16[512,256]{1,0:T(8,128)(2,1)}) custom-call(s32[128]{0:T(128)} %bitcast.16, s32[128]{0:T(128)} %bitcast.17, s32[128]{0:T(128)} %bitcast.18, s32[1,1]{1,0:T(1,128)S(6)} %copy.17.count, bf16[4,16,256]{2,1,0:T(8,128)(2,1)} %bitcast.14, bf16[8,128,256]{2,1,0:T(8,128)(2,1)} %bitcast.10, s32[128,128]{1,0:T(8,128)} %bitcast.11, ...), custom_call_target="tpu_custom_call" | custom-call | tf_op jit(solution)/shard_map/whole/pallas_call | solution.py:452
  135.1 0.0 copy-start
  135.1 2.3 %copy.18 = bf16[2048,256]{1,0:T(8,128)(2,1)} copy(bf16[2048,256]{1,0:T(8,128)(2,1)} %get-tuple-element.4) | data formatting | bytes 2097152
  137.4 0.0 copy-done
  137.4 0.7 copy.19
Async XLA Ops:
  135.1 2.3 %copy-start = (bf16[512,256]{1,0:T(8,128)(2,1)S(1)}, bf16[512,256]{1,0:T(8,128)(2,1)}, u32[]{:S(2)}) copy-start(bf16[512,256]{1,0:T(8,128)(2,1)} %get-tuple-element.5) | copy-start | bytes 786436

commit v5 on v4

--- a/solution.py
+++ b/solution.py
@@ -139,7 +139,7 @@
     xs = [neighbour(dx=d) for d in range(1, NX)]
     zs = [neighbour(dz=d) for d in range(1, NZ)]
     other = lax.rem(c + 1, 2)
-    barrier = greet([yp, ym, y2, sib] + xs + zs)
+    barrier = greet([yp, ym, y2, sib, zp, zm] + xs)
     go = Sender(send_sem, recv_sem)
     later = {}
     tab[0:4] = item_ref[...]
@@ -387,8 +387,8 @@
         copy.wait_recv()
     hg = back_z((yg[0] + yg[3]) + (yg[1] + yg[2]), outg)
     af = over_x(kf, pf, cf, sf, xf, 128)
+    bf = over_z(af, sf, xf, tf, zf, 8)
     ig = back_x(hg, outg)
-    bf = over_z(af, sf, xf, tf, zf, 8)
     back_c(ig, outg).wait_recv()
     for half in range(2):
         for i in range(NX):
@@ -412,6 +412,11 @@
     total = total + jnp.dot(outf[1].reshape(512, 128), inv[128:, :], preferred_element_type=F32, precision=HIGHEST)
     new[...] = total.astype(BF16)
     go.finish()
+
+
+def copy_kernel(uf, new, uf_out, new_out):
+    uf_out[...] = uf[...]
+    new_out[...] = new[...]
 
 
 VM = pl.BlockSpec(memory_space=pltpu.VMEM)
@@ -448,7 +453,7 @@
     profile,
     feature_factors,
 ):
-    return tuple(
+    uf, new = tuple(
         pl.pallas_call(
             whole_kernel,
             out_shape=(shape((SLAB, R), BF16), shape((512, R), BF16)),
@@ -500,6 +505,16 @@
             feature_factors,
         )
     )
+    return tuple(
+        pl.pallas_call(
+            copy_kernel,
+            out_shape=(shape((SLAB, R), BF16), shape((512, R), BF16)),
+            in_specs=[VM, VM],
+            out_specs=(VM, VM),
+            compiler_params=PLAIN,
+            name="results",
+        )(uf, new)
+    )
 
 
 def solution(mesh):

time: 138 us -> 134 us (0.971)
  local copies, waits for them, and re-layouts: 3.01 us -> 0 us
    pallas_call x1, Pallas kernels: 134 us -> 130 us  [local(): pl.pallas_call(whole_kernel, out_shape=(shape((SLAB, R), BF16), shape((51...]
    unnamed x4 -> x0, local copies, waits for them, and re-layouts: 3.01 us -> none
    pallas_call x0 -> x1, Pallas kernels: none -> 2.38 us  [local(): pl.pallas_call(copy_kernel, out_shape=(shape((SLAB, R), BF16), shape((512...]
where the time goes in v5:
time: 134 us
  Pallas kernels  133 us (99%)
    pallas_call x1, Pallas kernels, local(): pl.pallas_call(whole_kernel, out_shape=(shape((SLAB, R), BF16), shape((51...  130 us

profile of v5, /device:TPU:1, one launch (start us, length us, event | category | flops | bytes accessed | tf_op | source)
XLA Modules:
  0.0 134.0 jit_solution(4370677646471599704)
XLA Ops:
  1.3 130.4 %whole.1 = (bf16[2048,256]{1,0:T(8,128)(2,1)}, bf16[512,256]{1,0:T(8,128)(2,1)}) custom-call(s32[128]{0:T(128)} %bitcast.16, s32[128]{0:T(128)} %bitcast.17, s32[128]{0:T(128)} %bitcast.18, s32[1,1]{1,0:T(1,128)S(6)} %copy.15.count, bf16[4,16,256]{2,1,0:T(8,128)(2,1)} %bitcast.14, bf16[8,128,256]{2,1,0:T(8,128)(2,1)} %bitcast.10, s32[128,128]{1,0:T(8,128)} %bitcast.11, ...), custom_call_target="tpu_custom_call" | custom-call | tf_op jit(solution)/shard_map/whole/pallas_call | solution.py:457
  131.7 2.4 %results.1 = (bf16[2048,256]{1,0:T(8,128)(2,1)}, bf16[512,256]{1,0:T(8,128)(2,1)}) custom-call(bf16[2048,256]{1,0:T(8,128)(2,1)} %get-tuple-element.4.uf, bf16[512,256]{1,0:T(8,128)(2,1)} %get-tuple-element.5.new), custom_call_target="tpu_custom_call" | custom-call | tf_op jit(solution)/shard_map/results/pallas_call | solution.py:509

commit v6 on v5

--- a/solution.py
+++ b/solution.py
@@ -39,6 +39,13 @@
     for device in devices:
         pl.semaphore_signal(barrier, inc=1, device_id=device, device_id_type=MESH)
     return lambda: pl.semaphore_wait(barrier, len(devices))
+
+
+def farthest_first(n, start):
+    copies = {}
+    for d in sorted(range(1, n), key=lambda d: -min(d, n - d)):
+        copies[d] = start(d)
+    return [copies[d] for d in range(1, n)]
 
 
 class Sender:
@@ -330,7 +337,7 @@
     def over_x(k, part, came, held, slots, rows):
         k.wait_recv()
         held[...] = (part[c] + came[...]).reshape(NX, rows, 128)
-        return [go(held.at[lax.rem(x + d, NX)], slots.at[d - 1], xs[d - 1]) for d in range(1, NX)]
+        return farthest_first(NX, lambda d: go(held.at[lax.rem(x + d, NX)], slots.at[d - 1], xs[d - 1]))
 
     def over_z(copies, held, slots, split, zslots, rows):
         total = held[x]
@@ -339,7 +346,7 @@
             total = total + slots[d]
         for i in range(NZ):
             split[i] = total[i * rows : (i + 1) * rows, :]
-        return [go(split.at[lax.rem(z + d, NZ)], zslots.at[d - 1], zs[d - 1]) for d in range(1, NZ)]
+        return farthest_first(NZ, lambda d: go(split.at[lax.rem(z + d, NZ)], zslots.at[d - 1], zs[d - 1]))
 
     def sum_z(copies, split, zslots):
         total = split[z]
@@ -350,12 +357,12 @@
 
     def back_z(total, place):
         place[c, x, z] = total
-        return [go(place.at[c, x, z], place.at[c, x, z], zs[d - 1]) for d in range(1, NZ)]
+        return farthest_first(NZ, lambda d: go(place.at[c, x, z], place.at[c, x, z], zs[d - 1]))
 
     def back_x(copies, place):
         for copy in copies:
             copy.wait_recv()
-        return [go(place.at[c, x], place.at[c, x], xs[d - 1]) for d in range(1, NX)]
+        return farthest_first(NX, lambda d: go(place.at[c, x], place.at[c, x], xs[d - 1]))
 
     def back_c(copies, place):
         for copy in copies:
@@ -375,7 +382,7 @@
     um1.wait_recv()
     vm = go(out.at[bottom(after)], out.at[bottom(after)], ym)
     yg[0] = sum_z(bg, tg, zg)
-    hy = [go(yg.at[0], yg.at[1], yp), go(yg.at[0], yg.at[2], ym), go(yg.at[0], yg.at[3], y2)]
+    hy = [go(yg.at[0], yg.at[3], y2), go(yg.at[0], yg.at[1], yp), go(yg.at[0], yg.at[2], ym)]
     up1.wait_recv()
     vp.wait_recv()
     vm.wait_recv()

time: 134 us -> 133 us (level)
  Pallas kernels: 133 us -> 131 us
    pallas_call x1, Pallas kernels: 130 us -> 129 us  [local(): pl.pallas_call(whole_kernel, out_shape=(shape((SLAB, R), BF16), shape((51...]
where the time goes in v6:
time: 133 us
  Pallas kernels  131 us (98%)
    pallas_call x1, Pallas kernels, local(): pl.pallas_call(whole_kernel, out_shape=(shape((SLAB, R), BF16), shape((51...  129 us

profile of v6, /device:TPU:1, one launch (start us, length us, event | category | flops | bytes accessed | tf_op | source)
XLA Modules:
  0.0 132.5 jit_solution(1924104560296836017)
XLA Ops:
  1.3 128.9 %whole.1 = (bf16[2048,256]{1,0:T(8,128)(2,1)}, bf16[512,256]{1,0:T(8,128)(2,1)}) custom-call(s32[128]{0:T(128)} %bitcast.16, s32[128]{0:T(128)} %bitcast.17, s32[128]{0:T(128)} %bitcast.18, s32[1,1]{1,0:T(1,128)S(6)} %copy.15.count, bf16[4,16,256]{2,1,0:T(8,128)(2,1)} %bitcast.14, bf16[8,128,256]{2,1,0:T(8,128)(2,1)} %bitcast.10, s32[128,128]{1,0:T(8,128)} %bitcast.11, ...), custom_call_target="tpu_custom_call" | custom-call | tf_op jit(solution)/shard_map/whole/pallas_call | solution.py:464
  130.2 2.4 %results.1 = (bf16[2048,256]{1,0:T(8,128)(2,1)}, bf16[512,256]{1,0:T(8,128)(2,1)}) custom-call(bf16[2048,256]{1,0:T(8,128)(2,1)} %get-tuple-element.4.uf, bf16[512,256]{1,0:T(8,128)(2,1)} %get-tuple-element.5.new), custom_call_target="tpu_custom_call" | custom-call | tf_op jit(solution)/shard_map/results/pallas_call | solution.py:516
